TPU v7x, 512 devices: a whole 4x4x16 slice. The times are simulated.
512 devices in a mesh: lat: 32 (over y, z_lo), lon: 16 (over z_hi, x, core).
Axes of the slice: x: 4, y: 4, z: 16 (z_hi: 2, z_lo: 8; z = z_hi * 8 + z_lo), core: 2. Of those that a mesh axis runs over, the one named last changes fastest.
Arguments:
- field: bfloat16 [512, 512, 256], P('lat', 'lon'), may hold values from -6 to 6
- cotangent: bfloat16 [512, 512, 256], P('lat', 'lon'), may hold values from -6 to 6
- kernel: bfloat16 [9, 256, 256], replicated, may hold values from -0.125 to 0.125
- timestep: int32 [1], replicated, may hold values from 0 to 999
- time_weight: float32 [256, 256], replicated, may hold values from -0.375 to 0.375
- norm_gain: float32 [256], replicated, may hold values from 0.1 to 1.9
- w_query: bfloat16 [256, 256], replicated, may hold values from -1.5 to 1.5
- w_key: bfloat16 [256, 256], replicated, may hold values from -0.375 to 0.375
- w_value: bfloat16 [256, 256], replicated, may hold values from -0.375 to 0.375
- w_out: bfloat16 [256, 256], replicated, may hold values from -0.375 to 0.375
Outputs:
- block_out: bfloat16 [512, 512, 256], P('lat', 'lon')
- grad_field: bfloat16 [512, 512, 256], P('lat', 'lon')
- grad_kernel: float32 [9, 256, 256], P(None, 'lat', 'lon')
- attended: bfloat16 [64, 64, 256], P('lat', 'lon')
All inputs are finite; a program needn't handle non-finite values.
Results may differ from a plain program's by a relative error of at most 0.008.
Values may be sent and summed in bfloat16 or wider, within the bound.
A program may use at most 128 MiB of HBM per device.

v0:
```python
import math

import jax
import jax.numpy as jnp
from jax import lax
from jax.sharding import PartitionSpec as P

HEAD_DIM = 64
TE = 256
POOL = 8


def extended(cells, sides, width):
    for axis, dim in sides:
        count = lax.axis_size(axis)
        ends = count - 1
        head = lax.slice_in_dim(cells, 0, width, axis=dim)
        tail = lax.slice_in_dim(cells, cells.shape[dim] - width, cells.shape[dim], axis=dim)
        cells = jnp.concatenate(
            [
                lax.ppermute(tail, axis, [(i, (i + 1) % count) for i in range(ends)]),
                cells,
                lax.ppermute(head, axis, [((i + 1) % count, i) for i in range(ends)]),
            ],
            axis=dim,
        )
    return cells


def embed(timestep):
    half = TE // 2
    freqs = jnp.exp(-math.log(10000.0) * jnp.arange(half, dtype=jnp.float32) / half)
    angles = timestep.astype(jnp.float32)[:, None] * freqs[None, :]
    return jnp.concatenate([jnp.cos(angles), jnp.sin(angles)], axis=1)


def shards(
    field, cotangent, kernel, timestep, time_weight, norm_gain, w_query, w_key, w_value, w_out
):
    rows, cols, chans = field.shape
    xf = field.astype(jnp.float32)
    sig = jax.nn.sigmoid(xf)
    act = (xf * sig).astype(jnp.bfloat16)
    act_pad = extended(act, (("lat", 0), ("lon", 1)), 1)
    cot_pad = extended(cotangent, (("lat", 0), ("lon", 1)), 1)
    cot_flat = cotangent.reshape(-1, chans)
    conv = jnp.zeros((rows * cols, chans), jnp.float32)
    back = jnp.zeros((rows * cols, chans), jnp.float32)
    grads = []
    for row_off in range(3):
        for col_off in range(3):
            tap = row_off * 3 + col_off
            window = act_pad[row_off : row_off + rows, col_off : col_off + cols].reshape(-1, chans)
            conv = conv + jnp.dot(window, kernel[tap], preferred_element_type=jnp.float32)
            grads.append(
                lax.dot_general(
                    window, cot_flat, (((0,), (0,)), ((), ())), preferred_element_type=jnp.float32
                )
            )
            behind = cot_pad[
                2 - row_off : 2 - row_off + rows, 2 - col_off : 2 - col_off + cols
            ].reshape(-1, chans)
            back = back + lax.dot_general(
                behind, kernel[tap], (((1,), (1,)), ((), ())), preferred_element_type=jnp.float32
            )
    tbias = jnp.dot(embed(timestep), time_weight, precision=lax.Precision.HIGHEST)
    block_out = (xf + conv.reshape(rows, cols, chans) + tbias).astype(jnp.bfloat16)
    grad_field = (
        cotangent.astype(jnp.float32)
        + back.reshape(rows, cols, chans) * sig * (1.0 + xf * (1.0 - sig))
    ).astype(jnp.bfloat16)
    stacked = jnp.stack(grads)
    row_share = lax.psum_scatter(stacked, "lat", scatter_dimension=1, tiled=True)
    grad_kernel = lax.psum_scatter(row_share, "lon", scatter_dimension=2, tiled=True)
    tok_rows = rows // POOL
    tok_cols = cols // POOL
    pooled = (
        block_out.astype(jnp.float32)
        .reshape(tok_rows, POOL, tok_cols, POOL, chans)
        .mean(axis=(1, 3))
        .reshape(-1, chans)
    )
    center = pooled - jnp.mean(pooled, axis=1, keepdims=True)
    spread = jnp.mean(center * center, axis=1, keepdims=True)
    normed = (center * lax.rsqrt(spread + 1e-05) * norm_gain).astype(jnp.bfloat16)
    query = jnp.dot(normed, w_query, preferred_element_type=jnp.float32).astype(jnp.bfloat16)
    local_keys = jnp.dot(normed, w_key, preferred_element_type=jnp.float32).astype(jnp.bfloat16)
    local_values = jnp.dot(normed, w_value, preferred_element_type=jnp.float32).astype(jnp.bfloat16)
    joined = lax.all_gather(
        jnp.concatenate([local_keys, local_values], axis=1), ("lat", "lon"), axis=0, tiled=True
    )
    keys = joined[:, :chans]
    values = joined[:, chans:]
    heads = chans // HEAD_DIM
    q3 = query.reshape(-1, heads, HEAD_DIM)
    k3 = keys.reshape(-1, heads, HEAD_DIM)
    v3 = values.reshape(-1, heads, HEAD_DIM)
    scores = jnp.einsum("qhd,khd->hqk", q3, k3, preferred_element_type=jnp.float32) / math.sqrt(
        HEAD_DIM
    )
    probs = jax.nn.softmax(scores, axis=-1).astype(jnp.bfloat16)
    mixed = (
        jnp.einsum("hqk,khd->qhd", probs, v3, preferred_element_type=jnp.float32)
        .astype(jnp.bfloat16)
        .reshape(-1, chans)
    )
    attended = (
        (pooled + jnp.dot(mixed, w_out, preferred_element_type=jnp.float32))
        .astype(jnp.bfloat16)
        .reshape(tok_rows, tok_cols, chans)
    )
    return (block_out, grad_field, grad_kernel, attended)


def solution(mesh):
    in_specs = (
        P("lat", "lon", None),
        P("lat", "lon", None),
        P(),
        P(),
        P(),
        P(),
        P(),
        P(),
        P(),
        P(),
    )
    out_specs = (
        P("lat", "lon", None),
        P("lat", "lon", None),
        P(None, "lat", "lon"),
        P("lat", "lon", None),
    )
    return jax.shard_map(shards, mesh=mesh, in_specs=in_specs, out_specs=out_specs, check_vma=False)
```

profile of v0, /device:TPU:1, one launch (start us, length us, event | category | flops | bytes accessed | tf_op | source)
XLA Modules:
  0.0 1161.0 jit_solution(1753643822823815927)
XLA Ops:
  8.1 0.8 fusion.100
  8.9 1.3 collective-permute-start.5
  10.2 5.0 collective-permute-start.4
  15.2 1.1 fusion.20
  16.3 1.3 collective-permute-start.1
  17.6 4.2 collective-permute-start
  22.5 0.2 fusion.80
  22.8 1.3 pad_maximum_fusion.4
  24.2 8.7 collective-permute-start.6
  32.9 1.9 collective-permute-start.7
  34.8 0.3 fusion.42
  35.1 0.3 fusion.55
  35.4 1.9 collective-permute-start.2
  37.3 2.4 collective-permute-start.3
  39.7 0.7 pad_maximum_fusion.5
  40.5 1.0 fusion.57
  41.6 1.4 pad_maximum_fusion.3
  42.9 0.3 fusion.38
  43.2 0.2 maximum_maximum_fusion
  43.4 1.0 fusion.14
  44.4 1.2 fusion.97
  45.6 1.0 fusion.7
  46.6 1.0 fusion.13
  47.6 1.0 fusion.12
  48.6 1.0 fusion.11
  49.6 1.0 fusion.10
  50.6 1.0 fusion.9
  51.6 1.0 fusion.6
  52.6 1.0 fusion.8
  53.6 1.3 convolution_add_fusion.5
  54.9 1.2 convolution_add_fusion.4
  56.2 0.3 convolution_add_fusion.3
  56.5 0.2 fusion.40
  56.7 0.3 convolution_add_fusion.2
  57.1 0.3 convolution_add_fusion.1
  57.6 0.2 convolution_add_fusion.12
  57.8 0.2 convolution_add_fusion.11
  58.1 0.2 convolution_add_fusion.10
  58.4 0.2 convolution_add_fusion.9
  58.6 0.2 copy-done.7
  58.8 0.2 convolution_add_fusion.8
  59.1 0.2 convolution_add_fusion.7
  59.4 0.2 fusion.5
  59.6 0.2 copy-done.11
  59.8 0.3 fusion.4
  60.0 0.3 copy-done.13
  60.3 1.0 fusion.26
  61.5 0.2 multiply_reduce_fusion
  62.0 0.1 convolution_convert_fusion.3
  62.2 244.6 %reduce-scatter.5.cloned.1.call-done = f32[9,8,256]{2,1,0:T(8,128)} async-done(((f32[9,256,256]{2,1,0:T(8,128)}), f32[9,8,256]{2,1,0:T(8,128)}) %reduce-scatter.5.cloned.1.call-update) | async-done | bytes 73744 | tf_op jit(solution)/shard_map/reduce_scatter | solution.py:73
  306.8 2.1 copy.25
  308.9 1.2 reshape.202
  310.2 0.6 pad_maximum_fusion.10
  311.0 111.7 %reduce-scatter.7.cloned.1.call-done = f32[16,72]{1,0:T(8,128)} async-done(((f32[256,72]{1,0:T(8,128)}), f32[16,72]{1,0:T(8,128)}) %reduce-scatter.7.cloned.1.call-update) | async-done | bytes 4624
  422.7 0.8 reshape.203
  423.5 0.7 copy.26
  424.2 715.7 %all-gather.2.cloned.1.call-done = bf16[4096,512]{1,0:T(8,128)(2,1)} async-done(((bf16[8,512]{1,0:T(8,128)(2,1)}), bf16[4096,512]{1,0:T(8,128)(2,1)}) %all-gather.2.cloned.1.call-update) | async-done | bytes 4194320 | tf_op jit(solution)/shard_map/all_gather | solution.py:89
  1139.9 3.8 fusion.96
  1143.8 2.9 copy.21
  1146.7 2.9 copy.22
  1149.6 0.4 convolution_multiply_fusion
  1150.0 0.3 fusion.102
  1150.3 2.4 fusion.15
  1152.9 0.6 reshape.188
  (75 shorter events, 2.0 us)
Async XLA Ops:
  8.0 14.5 %copy-start = (f32[256,256]{1,0:T(8,128)S(1)}, f32[256,256]{1,0:T(8,128)}, u32[]{:S(2)}) copy-start(f32[256,256]{1,0:T(8,128)} %param.14) | copy-start | bytes 786436
  8.0 26.8 %copy-start.1 = (bf16[9,256,256]{2,1,0:T(8,128)(2,1)S(1)}, bf16[9,256,256]{2,1,0:T(8,128)(2,1)}, u32[]{:S(2)}) copy-start(bf16[9,256,256]{2,1,0:T(8,128)(2,1)} %param.12) | copy-start | bytes 3538948
  8.0 298.7 %reduce-scatter.5.cloned.1.call-start = ((), (), s32[]{:S(2)}) async-start(), calls=%async_computation.2 | async-start | bytes 2433024 | tf_op jit(solution)/shard_map/reduce_scatter | solution.py:73
  8.9 13.9 %collective-permute-start.5 = (bf16[1,32,256]{2,1,0:T(8,128)(2,1)S(1)}, bf16[1,32,256]{2,1,0:T(8,128)(2,1)S(1)}, u32[]{:S(2)}, u32[]{:S(2)}) collective-permute-start(bf16[1,32,256]{2,1,0:T(8,128)(2,1)S(1)} %get-tuple-element.32), channel_id=1, source_target_pairs={{16,0},{32,16},{48,32},{64,48},{80,64},{96,80},{112,96},{128,112},... | collective-permute-start | bytes 49160 | tf_op jit(solution)/shard_map/ppermute | solution.py:23
  10.2 12.5 %collective-permute-start.4 = (bf16[1,32,256]{2,1,0:T(8,128)(2,1)S(1)}, bf16[1,32,256]{2,1,0:T(8,128)(2,1)S(1)}, u32[]{:S(2)}, u32[]{:S(2)}) collective-permute-start(bf16[1,32,256]{2,1,0:T(8,128)(2,1)S(1)} %get-tuple-element.33), channel_id=1, source_target_pairs={{0,16},{16,32},{32,48},{48,64},{64,80},{80,96},{96,112},{112,128},... | collective-permute-start | bytes 49160 | tf_op jit(solution)/shard_map/ppermute | solution.py:21
  16.3 19.0 %collective-permute-start.1 = (bf16[1,32,256]{2,1,0:T(8,128)(2,1)S(1)}, bf16[1,32,256]{2,1,0:T(8,128)(2,1)S(1)}, u32[]{:S(2)}, u32[]{:S(2)}) collective-permute-start(bf16[1,32,256]{2,1,0:T(8,128)(2,1)S(1)} %get-tuple-element.37), channel_id=1, source_target_pairs={{16,0},{32,16},{48,32},{64,48},{80,64},{96,80},{112,96},{128,112},... | collective-permute-start | bytes 49160 | tf_op jit(solution)/shard_map/ppermute | solution.py:23
  17.6 17.7 %collective-permute-start = (bf16[1,32,256]{2,1,0:T(8,128)(2,1)S(1)}, bf16[1,32,256]{2,1,0:T(8,128)(2,1)S(1)}, u32[]{:S(2)}, u32[]{:S(2)}) collective-permute-start(bf16[1,32,256]{2,1,0:T(8,128)(2,1)S(1)} %get-tuple-element.36), channel_id=1, source_target_pairs={{0,16},{16,32},{32,48},{48,64},{64,80},{80,96},{96,112},{112,128},... | collective-permute-start | bytes 49160 | tf_op jit(solution)/shard_map/ppermute | solution.py:21
  24.2 17.4 %collective-permute-start.6 = (bf16[18,1,256]{2,1,0:T(2,128)(2,1)S(1)}, bf16[18,1,256]{2,1,0:T(2,128)(2,1)S(1)}, u32[]{:S(2)}, u32[]{:S(2)}) collective-permute-start(bf16[18,1,256]{2,1,0:T(2,128)(2,1)S(1)} %get-tuple-element.21), channel_id=1, source_target_pairs={{1,0},{2,1},{3,2},{4,3},{5,4},{6,5},{7,6},{8,7},{9,8},{10,9},{11,1... | collective-permute-start | bytes 27656 | tf_op jit(solution)/shard_map/ppermute | solution.py:23
  32.9 8.7 collective-permute-start.7
  35.4 7.8 collective-permute-start.2
  37.3 5.9 collective-permute-start.3
  41.5 1.9 copy-start.2
  46.6 2.0 copy-start.12
  53.6 369.1 %reduce-scatter.7.cloned.1.call-start = ((), (), s32[]{:S(2)}) async-start(), calls=%async_computation.4 | async-start | bytes 139264
  53.6 2.5 copy-start.16
  53.6 2.8 copy-start.5
  56.1 1.0 copy-start.15
  56.4 1.1 copy-start.3
  56.4 1.1 copy-start.10
  56.7 1.1 copy-start.9
  57.1 1.0 copy-start.8
  57.8 1.0 copy-start.7
  58.1 1.0 copy-start.6
  58.4 1.0 copy-start.4
  58.8 1.0 copy-start.11
  59.4 1.0 copy-start.13
  59.8 2.0 copy-start.21
  59.8 2.1 copy-start.18
  59.8 2.2 copy-start.19
  61.3 248.8 %copy-start.14 = (bf16[16,32,256]{2,1,0:T(8,128)(2,1)}, bf16[16,32,256]{2,1,0:T(8,128)(2,1)S(1)}, u32[]{:S(2)}) copy-start(bf16[16,32,256]{2,1,0:T(8,128)(2,1)S(1)} %get-tuple-element.28) | copy-start | bytes 786436
  62.2 248.6 %copy-start.20 = (bf16[256,256]{1,0:T(8,128)(2,1)S(1)}, bf16[256,256]{1,0:T(8,128)(2,1)}, u32[]{:S(2)}) copy-start(bf16[256,256]{1,0:T(8,128)(2,1)} %param.16) | copy-start | bytes 393220
  310.1 829.8 %all-gather.2.cloned.1.call-start = ((), (), s32[]{:S(2)}) async-start(), calls=%async_computation.3 | async-start | bytes 4202496 | tf_op jit(solution)/shard_map/all_gather | solution.py:89
  1150.3 2.5 copy-start.17
Sparse Core Ops, SparseCore 0:
  53.7 253.0 reduce-scatter.4
  311.3 111.3 reduce-scatter.6
Sparse Core Ops, SparseCore 1:
  313.0 826.9 all-gather.1
where the time goes:
time: 1170 us; the launch traced here: 1160 us
  waiting for transfers between devices  1070 us (91%)
  starting transfers between devices  26.8 us (2%)
  matrix products  19.6 us (2%)
  local copies, waits for them, and re-layouts  18.8 us (2%)
  between operations  16.6 us (1%)
    all_gather x1, waiting for transfers between devices, shards(): lax.all_gather(jnp.concatenate([local_keys, local_values], axis=1), ('lat...  716 us
    reduce_scatter x1, waiting for transfers between devices, shards(): lax.psum_scatter(stacked, 'lat', scatter_dimension=1, tiled=True)  245 us
    unnamed x4, waiting for transfers between devices  112 us
  transfers between devices with their start and end apart: 11, of which 3 were waited for; matrix products, arithmetic and copies ran while one was open for 1% of the time, Pallas kernels for 0%

commit v1 on v0

v1 whole, which is shorter than its diff:
```python
import functools
import math

import jax
import jax.numpy as jnp
from jax import lax
from jax.experimental import pallas as pl
from jax.experimental.pallas import tpu as pltpu
from jax.sharding import PartitionSpec as P

HEAD_DIM = 64
TE = 256
POOL = 8
MESH = pl.DeviceIdType.MESH
F32 = jnp.float32
BF16 = jnp.bfloat16

NY, NZ, NX, NC = 4, 16, 4, 2
ROWS, COLS, C = 16, 32, 256
CELLS = ROWS * COLS
PLANE = [
    (dy, dx, dc) for dy in range(NY) for dx in range(NX) for dc in range(NC) if (dy, dx, dc) != (0, 0, 0)
]
NPLANE = len(PLANE)
NRING = NZ - 1


def device(y, z, x, c):
    return (y * 8 + z % 8, (z // 8) * 8 + x * 2 + c)


def dot(a, b):
    return jnp.dot(a, b, preferred_element_type=F32)


def dot_t(a, b):
    return lax.dot_general(a, b, (((1,), (1,)), ((), ())), preferred_element_type=F32)


def silu_rounded(v):
    return (v / (1.0 + jnp.exp(-v))).astype(BF16).astype(F32)


def send(src, dst, send_sem, recv_sem, dev):
    pltpu.make_async_remote_copy(
        src_ref=src,
        dst_ref=dst,
        send_sem=send_sem,
        recv_sem=recv_sem,
        device_id=dev,
        device_id_type=MESH,
    ).start()


def await_recv(buf, send_sem, recv_sem, dev):
    pltpu.make_async_remote_copy(
        src_ref=buf,
        dst_ref=buf,
        send_sem=send_sem,
        recv_sem=recv_sem,
        device_id=dev,
        device_id_type=MESH,
    ).wait_recv()


def await_send(buf, send_sem, recv_sem, dev):
    pltpu.make_async_remote_copy(
        src_ref=buf,
        dst_ref=buf,
        send_sem=send_sem,
        recv_sem=recv_sem,
        device_id=dev,
        device_id_type=MESH,
    ).wait_send()


def embed_bias(step, time_weight):
    half = TE // 2
    index = lax.broadcasted_iota(jnp.int32, (8, half), 1).astype(F32)
    freqs = jnp.exp(-math.log(10000.0) * index / half)
    angles = step.astype(F32) * freqs
    emb = jnp.concatenate([jnp.cos(angles), jnp.sin(angles)], axis=1)
    full = jnp.dot(emb, time_weight, precision=lax.Precision.HIGHEST, preferred_element_type=F32)
    return full[0:1, :]


def body(
    step_ref, field, cot, taps, time_weight, gain, w_query, w_key, w_value, w_out,
    block_out, grad_field, grad_kernel, attended,
    col_out, cor_out, row_in, col_in, cor_in,
    pad_act, pad_cot, win_act, win_cot,
    grads, core_in, core_sum, x_in, y_out, y_in, z_out, z_in,
    q_buf, kv_buf, part_out, part_in,
    halo_s, halo_r, group_s, group_r,
):
    lat, lon = lax.axis_index("lat"), lax.axis_index("lon")
    y, x, core = lat // 8, (lon // 2) % 4, lon % 2
    z = (lon // 8) * 8 + lat % 8

    def plane(k, sign):
        dy, dx, dc = PLANE[k]
        return device((y + sign * dy + NY) % NY, z, (x + sign * dx + NX) % NX, (core + dc) % NC)

    def ring(dz):
        return device(y, (z + dz + NZ) % NZ, x, core)

    up, down = (lat + 31) % 32, (lat + 1) % 32
    left, right = (lon + 15) % 16, (lon + 1) % 16
    corners = [(up, left), (up, right), (down, left), (down, right)]
    near = [(up, lon), (down, lon), (lat, left), (lat, right)] + corners
    other = (lat, lon + 1 - 2 * core)

    barrier = pltpu.get_barrier_semaphore()
    everyone = near + [plane(k, 1) for k in range(NPLANE)] + [ring(d) for d in range(1, NZ)]
    for dev in everyone:
        pl.semaphore_signal(barrier, inc=1, device_id=dev, device_id_type=MESH)

    cell = lax.broadcasted_iota(jnp.int32, (32, CELLS), 1)
    line = lax.broadcasted_iota(jnp.int32, (32, CELLS), 0)
    edge_cell = (line % 16) * COLS + (line // 16) * (COLS - 1)
    pick = jnp.where(cell == edge_cell, 1.0, 0.0).astype(BF16)
    flat_field = field[...].reshape(CELLS, C)
    flat_cot = cot[...].reshape(CELLS, C)
    field_cols = dot(pick, flat_field).astype(BF16)
    cot_cols = dot(pick, flat_cot).astype(BF16)
    col_out[0, 0:16, :] = field_cols[0:16]
    col_out[0, 16:32, :] = cot_cols[0:16]
    col_out[1, 0:16, :] = field_cols[16:32]
    col_out[1, 16:32, :] = cot_cols[16:32]
    corner = line // 8
    corner_cell = (corner // 2) * (CELLS - COLS) + (corner % 2) * (COLS - 1)
    pick_field = jnp.where((cell == corner_cell) & (line % 8 == 0), 1.0, 0.0).astype(BF16)
    pick_cot = jnp.where((cell == corner_cell) & (line % 8 == 1), 1.0, 0.0).astype(BF16)
    cor_out[...] = (dot(pick_field, flat_field) + dot(pick_cot, flat_cot)).reshape(4, 8, C)

    pl.semaphore_wait(barrier, len(everyone))

    sends = [
        (field.at[ROWS - 1], row_in.at[0, 0], (down, lon)),
        (cot.at[ROWS - 1], row_in.at[0, 1], (down, lon)),
        (field.at[0], row_in.at[1, 0], (up, lon)),
        (cot.at[0], row_in.at[1, 1], (up, lon)),
        (col_out.at[1], col_in.at[0], (lat, right)),
        (col_out.at[0], col_in.at[1], (lat, left)),
        (cor_out.at[3], cor_in.at[0], corners[3]),
        (cor_out.at[2], cor_in.at[1], corners[2]),
        (cor_out.at[1], cor_in.at[2], corners[1]),
        (cor_out.at[0], cor_in.at[3], corners[0]),
    ]
    copies = []
    for i, (src, dst, dev) in enumerate(sends):
        copy = pltpu.make_async_remote_copy(
            src_ref=src, dst_ref=dst, send_sem=halo_s.at[i], recv_sem=halo_r.at[i],
            device_id=dev, device_id_type=MESH,
        )
        copy.start()
        copies.append(copy)

    xf = flat_field.astype(F32)
    pad_act[1 : ROWS + 1, 8 : 8 + COLS, :] = silu_rounded(xf).reshape(ROWS, COLS, C)
    pad_cot[1 : ROWS + 1, 8 : 8 + COLS, :] = flat_cot.astype(F32).reshape(ROWS, COLS, C)
    tbias = embed_bias(step_ref[0], time_weight[...])
    row = lax.broadcasted_iota(jnp.int32, (C, C), 0)
    col = lax.broadcasted_iota(jnp.int32, (C, C), 1)
    source = (((row // 16) % 2) * 8 + ((row // 32) % 4) * 2 + row // 128) * 16 + row % 16
    reorder = jnp.where(col == source, 1.0, 0.0).astype(BF16)
    cot_t = dot_t(reorder, flat_cot).astype(BF16)

    for copy in copies:
        copy.wait_recv()
    has_up = jnp.where(lat > 0, 1.0, 0.0)
    has_down = jnp.where(lat < 31, 1.0, 0.0)
    has_left = jnp.where(lon > 0, 1.0, 0.0)
    has_right = jnp.where(lon < 15, 1.0, 0.0)
    for end, (r, has) in enumerate(((0, has_up), (ROWS + 1, has_down))):
        pad_act[r, 8 : 8 + COLS, :] = silu_rounded(row_in[end, 0].astype(F32) * has)
        pad_cot[r, 8 : 8 + COLS, :] = row_in[end, 1].astype(F32) * has
    for side, (j, has) in enumerate(((7, has_left), (8 + COLS, has_right))):
        edge = col_in[side].astype(F32) * has
        act_edge = silu_rounded(edge[0:16])
        for r in range(ROWS):
            pad_act[r + 1, j : j + 1, :] = act_edge[r : r + 1]
            pad_cot[r + 1, j : j + 1, :] = edge[16 + r : 17 + r]
    for i, (r, j, has) in enumerate((
        (0, 7, has_up * has_left),
        (0, 8 + COLS, has_up * has_right),
        (ROWS + 1, 7, has_down * has_left),
        (ROWS + 1, 8 + COLS, has_down * has_right),
    )):
        edge = cor_in[i] * has
        pad_act[r, j : j + 1, :] = silu_rounded(edge[0:1])
        pad_cot[r, j : j + 1, :] = edge[1:2]

    for b in range(3):
        win_act[b] = pad_act[:, 7 + b : 7 + b + COLS, :].astype(BF16)

    def window(ref, a, b):
        return ref[b, a : a + ROWS].reshape(CELLS, C)

    conv = xf + tbias
    for tap in range(9):
        conv = conv + dot(window(win_act, tap // 3, tap % 3), taps[tap])
    rounded = conv.astype(BF16)
    block_out[...] = rounded.reshape(ROWS, COLS, C)

    token = lax.broadcasted_iota(jnp.int32, (8, CELLS), 0)
    cell8 = lax.broadcasted_iota(jnp.int32, (8, CELLS), 1)
    its_token = (cell8 // (COLS * POOL)) * 4 + (cell8 % COLS) // POOL
    pooled = dot(jnp.where(token == its_token, 1.0, 0.0).astype(BF16), rounded) * (1.0 / (POOL * POOL))
    center = pooled - jnp.mean(pooled, axis=1, keepdims=True)
    spread = jnp.mean(center * center, axis=1, keepdims=True)
    normed = (center * lax.rsqrt(spread + 1e-05) * gain[...]).astype(BF16)
    query = dot(normed, w_query[...])
    keys = dot(normed, w_key[...])
    values = dot(normed, w_value[...])
    q_buf[NPLANE] = jnp.concatenate([query[:, 0:128], query[:, 128:256]], axis=0).astype(BF16)
    kv_buf[NRING] = jnp.concatenate([keys, values], axis=0).astype(BF16)
    for d in range(1, NZ):
        send(kv_buf.at[NRING], kv_buf.at[d - 1], group_s.at[0], group_r.at[0], ring(d))
    for k in range(NPLANE):
        send(q_buf.at[NPLANE], q_buf.at[k], group_s.at[1], group_r.at[1], plane(k, 1))

    for tap in range(9):
        part = dot(cot_t, window(win_act, tap // 3, tap % 3)).astype(BF16)
        grads[:, :, tap] = part.reshape(2, 4, 32, C)
    send(grads.at[1 - core], core_in, group_s.at[2], group_r.at[2], other)

    for b in range(3):
        win_cot[b] = pad_cot[:, 7 + b : 7 + b + COLS, :].astype(BF16)
    back = jnp.zeros((CELLS, C), F32)
    for tap in range(9):
        back = back + dot_t(window(win_cot, 2 - tap // 3, 2 - tap % 3), taps[tap])
    sig = 1.0 / (1.0 + jnp.exp(-xf))
    grad_field[...] = (
        (flat_cot.astype(F32) + back * sig * (1.0 + xf * (1.0 - sig))).astype(BF16).reshape(ROWS, COLS, C)
    )

    await_recv(core_in, group_s.at[2], group_r.at[2], other)
    core_sum[...] = (grads[core].astype(F32) + core_in[...].astype(F32)).astype(BF16)
    for k in range(1, NX):
        to = (x + k) % NX
        send(core_sum.at[to], x_in.at[k - 1], group_s.at[3], group_r.at[3], device(y, z, to, core))

    await_recv(kv_buf.at[0:NRING], group_s.at[0], group_r.at[0], other)
    await_recv(q_buf.at[0:NPLANE], group_s.at[1], group_r.at[1], other)
    nq, nk = 8 * (NPLANE + 1), 8 * NZ
    q32 = q_buf[...].astype(F32)
    kv32 = kv_buf[...].astype(F32)
    all_k = kv32[:, 0:8, :].reshape(nk, C).astype(BF16)
    all_v = kv32[:, 8:16, :].reshape(nk, C).astype(BF16)
    lane_q = lax.broadcasted_iota(jnp.int32, (nq, 128), 1)
    lane_k = lax.broadcasted_iota(jnp.int32, (nk, 128), 1)
    lse = jnp.zeros((nq, 128), F32)
    for pair in range(2):
        q2 = q32[:, 8 * pair : 8 * pair + 8, :].reshape(nq, 128)
        k2 = all_k[:, 128 * pair : 128 * pair + 128]
        v2 = all_v[:, 128 * pair : 128 * pair + 128].astype(F32)
        mixed2 = jnp.zeros((nq, 128), F32)
        for h in range(2):
            qm = jnp.where(lane_q // HEAD_DIM == h, q2, 0.0).astype(BF16)
            vm = jnp.where(lane_k // HEAD_DIM == h, v2, 0.0).astype(BF16)
            scores = dot_t(qm, k2) * (1.0 / math.sqrt(HEAD_DIM))
            top = jnp.max(scores, axis=1, keepdims=True)
            probs = jnp.exp(scores - top)
            total = jnp.sum(probs, axis=1, keepdims=True)
            mixed2 = mixed2 + dot(probs.astype(BF16), vm) * (1.0 / total)
            lse = jnp.where(lane_q // 32 == 2 * pair + h, top + jnp.log(total), lse)
        part_out[:, :, 128 * pair : 128 * pair + 128] = mixed2.reshape(NPLANE + 1, 8, 128)
    part_out[:, :, 256:384] = lse.reshape(NPLANE + 1, 8, 128)
    for k in range(NPLANE):
        send(part_out.at[k], part_in.at[k], group_s.at[4], group_r.at[4], plane(k, -1))

    await_recv(x_in, group_s.at[3], group_r.at[3], other)
    acc = core_sum[x].astype(F32)
    for k in range(NX - 1):
        acc = acc + x_in[k].astype(F32)
    lane = lax.broadcasted_iota(jnp.int32, (9 * 16, 128), 1)
    for t in range(2):
        low = acc[:, 0:16, 128 * t : 128 * t + 128].reshape(9 * 16, 128)
        high = acc[:, 16:32, 128 * t : 128 * t + 128].reshape(9 * 16, 128)
        even = jnp.where(lane < 64, low, pltpu.roll(high, 64, 1))
        odd = jnp.where(lane < 64, pltpu.roll(low, 64, 1), high)
        y_out[2 * t] = even.astype(BF16)
        y_out[2 * t + 1] = odd.astype(BF16)
    for k in range(1, NY):
        to = (y + k) % NY
        send(y_out.at[to], y_in.at[k - 1], group_s.at[5], group_r.at[5], device(to, z, x, core))

    await_recv(y_in, group_s.at[5], group_r.at[5], other)
    acc = y_out[y].astype(F32)
    for k in range(NY - 1):
        acc = acc + y_in[k].astype(F32)
    acc = jnp.concatenate([acc, jnp.zeros((256 - 144, 128), F32)], axis=0)
    z_out[...] = acc.T.reshape(NZ, 8, 256)
    for d in range(1, NZ):
        send(z_out.at[(z + d) % NZ], z_in.at[d - 1], group_s.at[6], group_r.at[6], ring(d))

    await_recv(part_in, group_s.at[4], group_r.at[4], other)
    lse = jnp.concatenate([part_in[:, :, 256:384], part_out[NPLANE:, :, 256:384]], axis=0)
    top = jnp.max(lse, axis=0, keepdims=True)
    share = jnp.exp(lse - top)
    share = (share / jnp.sum(share, axis=0, keepdims=True)).reshape(nq, 128)
    halves = []
    for pair in range(2):
        part = jnp.concatenate(
            [
                part_in[:, :, 128 * pair : 128 * pair + 128],
                part_out[NPLANE:, :, 128 * pair : 128 * pair + 128],
            ],
            axis=0,
        )
        first = share[:, 64 * pair : 64 * pair + 1]
        second = share[:, 64 * pair + 32 : 64 * pair + 33]
        weight = jnp.where(lane_q < 64, first, second).reshape(NPLANE + 1, 8, 128)
        halves.append(jnp.sum(part * weight, axis=0))
    mixed = jnp.concatenate(halves, axis=1).astype(BF16)
    attended[...] = (pooled + dot(mixed, w_out[...])).astype(BF16)

    await_recv(z_in, group_s.at[6], group_r.at[6], other)
    acc = z_out[z]
    for k in range(NRING):
        acc = acc + z_in[k]
    for tap in range(9):
        grad_kernel[tap] = acc[:, 16 * tap : 16 * tap + 16]

    for copy in copies:
        copy.wait_send()
    for i, buf in enumerate((kv_buf.at[0:NRING], q_buf.at[0:NPLANE], core_in, x_in, part_in, y_in, z_in)):
        await_send(buf, group_s.at[i], group_r.at[i], other)


def shards(
    field, cotangent, kernel, timestep, time_weight, norm_gain, w_query, w_key, w_value, w_out
):
    vmem = pl.BlockSpec(memory_space=pltpu.VMEM)
    call = pl.pallas_call(
        body,
        out_shape=(
            jax.ShapeDtypeStruct((ROWS, COLS, C), BF16),
            jax.ShapeDtypeStruct((ROWS, COLS, C), BF16),
            jax.ShapeDtypeStruct((9, 8, 16), F32),
            jax.ShapeDtypeStruct((8, C), BF16),
        ),
        in_specs=[pl.BlockSpec(memory_space=pltpu.SMEM)] + [vmem] * 9,
        out_specs=(vmem,) * 4,
        scratch_shapes=[
            pltpu.VMEM((2, 32, C), BF16),
            pltpu.VMEM((4, 8, C), F32),
            pltpu.VMEM((2, 2, COLS, C), BF16),
            pltpu.VMEM((2, 32, C), BF16),
            pltpu.VMEM((4, 8, C), F32),
            pltpu.VMEM((ROWS + 2, COLS + 16, C), F32),
            pltpu.VMEM((ROWS + 2, COLS + 16, C), F32),
            pltpu.VMEM((3, ROWS + 2, COLS, C), BF16),
            pltpu.VMEM((3, ROWS + 2, COLS, C), BF16),
            pltpu.VMEM((2, 4, 9, 32, C), BF16),
            pltpu.VMEM((4, 9, 32, C), BF16),
            pltpu.VMEM((4, 9, 32, C), BF16),
            pltpu.VMEM((NX - 1, 9, 32, C), BF16),
            pltpu.VMEM((NY, 144, 128), BF16),
            pltpu.VMEM((NY - 1, 144, 128), BF16),
            pltpu.VMEM((NZ, 8, 256), F32),
            pltpu.VMEM((NRING, 8, 256), F32),
            pltpu.VMEM((NPLANE + 1, 16, 128), BF16),
            pltpu.VMEM((NZ, 16, C), BF16),
            pltpu.VMEM((NPLANE + 1, 8, 384), F32),
            pltpu.VMEM((NPLANE, 8, 384), F32),
            pltpu.SemaphoreType.DMA((10,)),
            pltpu.SemaphoreType.DMA((10,)),
            pltpu.SemaphoreType.DMA((7,)),
            pltpu.SemaphoreType.DMA((7,)),
        ],
        compiler_params=pltpu.CompilerParams(
            collective_id=0, has_side_effects=True, vmem_limit_bytes=48 * 1024 * 1024
        ),
    )
    block_out, grad_field, grad_kernel, attended = call(
        timestep, field, cotangent, kernel, time_weight, norm_gain.reshape(1, C),
        w_query, w_key, w_value, w_out,
    )
    return block_out, grad_field, grad_kernel, attended.reshape(ROWS // POOL, COLS // POOL, C)


def solution(mesh):
    across = P("lat", "lon", None)
    return jax.shard_map(
        shards,
        mesh=mesh,
        in_specs=(across, across) + (P(),) * 8,
        out_specs=(across, across, P(None, "lat", "lon"), across),
        check_vma=False,
    )
```

time: 1170 us -> 70.9 us (0.06)
  the two profiles are of different devices: /device:TPU:1 before, /device:TPU:4 now
where the time goes in v1:
time: 70.9 us; the launch traced here: 70.6 us
  Pallas kernels  58.2 us (82%)
  local copies, waits for them, and re-layouts  11 us (16%)
  between operations  1.31 us (2%)
    pallas_call x1, Pallas kernels, shards(): call(timestep, field, cotangent, kernel, time_weight, norm_gain.reshape(1...  58.2 us
    unnamed x21, local copies, waits for them, and re-layouts  10.4 us

profile of v1, /device:TPU:4, one launch (start us, length us, event | category | flops | bytes accessed | tf_op | source)
XLA Modules:
  0.0 70.6 jit_solution(4086949145105132490)
XLA Ops:
  1.3 0.0 copy-start
  1.3 1.3 %copy-done = bf16[9,256,256]{2,1,0:T(8,128)(2,1)S(1)} copy-done((bf16[9,256,256]{2,1,0:T(8,128)(2,1)S(1)}, bf16[9,256,256]{2,1,0:T(8,128)(2,1)}, u32[]{:S(2)}) %copy-start) | copy-done | bytes 1179672
  2.6 0.0 copy-start.1
  2.6 0.9 %copy-done.1 = bf16[16,32,256]{2,1,0:T(8,128)(2,1)S(1)} copy-done((bf16[16,32,256]{2,1,0:T(8,128)(2,1)S(1)}, bf16[16,32,256]{2,1,0:T(8,128)(2,1)}, u32[]{:S(2)}) %copy-start.1) | copy-done | bytes 262168
  3.5 0.0 copy-start.2
  3.5 0.9 %copy-done.2 = bf16[16,32,256]{2,1,0:T(8,128)(2,1)S(1)} copy-done((bf16[16,32,256]{2,1,0:T(8,128)(2,1)S(1)}, bf16[16,32,256]{2,1,0:T(8,128)(2,1)}, u32[]{:S(2)}) %copy-start.2) | copy-done | bytes 262168
  4.5 0.0 copy-start.3
  4.5 0.9 %copy-done.3 = f32[256,256]{1,0:T(8,128)S(1)} copy-done((f32[256,256]{1,0:T(8,128)S(1)}, f32[256,256]{1,0:T(8,128)}, u32[]{:S(2)}) %copy-start.3) | copy-done | bytes 262168
  5.4 0.0 copy-start.4
  5.4 0.9 %copy-done.4 = bf16[256,256]{1,0:T(8,128)(2,1)S(1)} copy-done((bf16[256,256]{1,0:T(8,128)(2,1)S(1)}, bf16[256,256]{1,0:T(8,128)(2,1)}, u32[]{:S(2)}) %copy-start.4) | copy-done | bytes 131096
  6.3 0.0 copy-start.5
  6.3 0.9 %copy-done.5 = bf16[256,256]{1,0:T(8,128)(2,1)S(1)} copy-done((bf16[256,256]{1,0:T(8,128)(2,1)S(1)}, bf16[256,256]{1,0:T(8,128)(2,1)}, u32[]{:S(2)}) %copy-start.5) | copy-done | bytes 131096
  7.2 0.0 copy-start.6
  7.2 0.9 %copy-done.6 = bf16[256,256]{1,0:T(8,128)(2,1)S(1)} copy-done((bf16[256,256]{1,0:T(8,128)(2,1)S(1)}, bf16[256,256]{1,0:T(8,128)(2,1)}, u32[]{:S(2)}) %copy-start.6) | copy-done | bytes 131096
  8.1 0.0 copy-start.7
  8.1 0.9 %copy-done.7 = bf16[256,256]{1,0:T(8,128)(2,1)S(1)} copy-done((bf16[256,256]{1,0:T(8,128)(2,1)S(1)}, bf16[256,256]{1,0:T(8,128)(2,1)}, u32[]{:S(2)}) %copy-start.7) | copy-done | bytes 131096
  9.0 0.0 copy-start.8
  9.0 0.7 copy-done.8
  9.7 58.2 %shard_map.129 = (bf16[16,32,256]{2,1,0:T(8,128)(2,1)S(1)}, bf16[16,32,256]{2,1,0:T(8,128)(2,1)S(1)}, f32[9,8,16]{2,1,0:T(8,128)S(1)}, bf16[8,256]{1,0:T(8,128)(2,1)S(1)}) custom-call(s32[1]{0:T(128)S(6)} %copy.17.step_ref, bf16[16,32,256]{2,1,0:T(8,128)(2,1)S(1)} %copy-done.1, bf16[16,32,256]{2,1,0:T(8,128)(2,1)S(1)} %copy-done.2, ...), custom_call_target="tpu_custom_call" | custom-call | tf_op jit(solution)/shard_map/pallas_call | solution.py:377
  68.0 0.6 reshape.15
  68.6 0.7 copy.18
  69.3 0.7 copy.19
  70.0 0.6 copy.20
Async XLA Ops:
  1.3 1.3 %copy-start = (bf16[9,256,256]{2,1,0:T(8,128)(2,1)S(1)}, bf16[9,256,256]{2,1,0:T(8,128)(2,1)}, u32[]{:S(2)}) copy-start(bf16[9,256,256]{2,1,0:T(8,128)(2,1)} %taps.1) | copy-start | bytes 3538948
  2.6 0.9 %copy-start.1 = (bf16[16,32,256]{2,1,0:T(8,128)(2,1)S(1)}, bf16[16,32,256]{2,1,0:T(8,128)(2,1)}, u32[]{:S(2)}) copy-start(bf16[16,32,256]{2,1,0:T(8,128)(2,1)} %field.1) | copy-start | bytes 786436
  3.5 0.9 %copy-start.2 = (bf16[16,32,256]{2,1,0:T(8,128)(2,1)S(1)}, bf16[16,32,256]{2,1,0:T(8,128)(2,1)}, u32[]{:S(2)}) copy-start(bf16[16,32,256]{2,1,0:T(8,128)(2,1)} %cot.1) | copy-start | bytes 786436
  4.5 0.9 %copy-start.3 = (f32[256,256]{1,0:T(8,128)S(1)}, f32[256,256]{1,0:T(8,128)}, u32[]{:S(2)}) copy-start(f32[256,256]{1,0:T(8,128)} %time_weight.1) | copy-start | bytes 786436
  5.4 0.9 %copy-start.4 = (bf16[256,256]{1,0:T(8,128)(2,1)S(1)}, bf16[256,256]{1,0:T(8,128)(2,1)}, u32[]{:S(2)}) copy-start(bf16[256,256]{1,0:T(8,128)(2,1)} %w_query.1) | copy-start | bytes 393220
  6.3 0.9 %copy-start.5 = (bf16[256,256]{1,0:T(8,128)(2,1)S(1)}, bf16[256,256]{1,0:T(8,128)(2,1)}, u32[]{:S(2)}) copy-start(bf16[256,256]{1,0:T(8,128)(2,1)} %w_key.1) | copy-start | bytes 393220
  7.2 0.9 %copy-start.6 = (bf16[256,256]{1,0:T(8,128)(2,1)S(1)}, bf16[256,256]{1,0:T(8,128)(2,1)}, u32[]{:S(2)}) copy-start(bf16[256,256]{1,0:T(8,128)(2,1)} %w_value.1) | copy-start | bytes 393220
  8.1 0.9 %copy-start.7 = (bf16[256,256]{1,0:T(8,128)(2,1)S(1)}, bf16[256,256]{1,0:T(8,128)(2,1)}, u32[]{:S(2)}) copy-start(bf16[256,256]{1,0:T(8,128)(2,1)} %w_out.1) | copy-start | bytes 393220
  9.0 0.7 copy-start.8

commit v2 on v1

--- a/solution.py
+++ b/solution.py
@@ -21,7 +21,9 @@
 PLANE = [
     (dy, dx, dc) for dy in range(NY) for dx in range(NX) for dc in range(NC) if (dy, dx, dc) != (0, 0, 0)
 ]
+PLANE.sort(key=lambda d: -(min(d[0], NY - d[0]) + min(d[1], NX - d[1]) + 0.5 * d[2]))
 NPLANE = len(PLANE)
+RING = sorted(range(1, NZ), key=lambda d: -min(d, NZ - d))
 NRING = NZ - 1
 
 
@@ -85,14 +87,30 @@
 
 
 def body(
-    step_ref, field, cot, taps, time_weight, gain, w_query, w_key, w_value, w_out,
+    step_ref, field_hbm, cot_hbm, taps_hbm, time_weight_hbm, gain_hbm, w_query_hbm, w_key_hbm, w_value_hbm,
+    w_out_hbm,
     block_out, grad_field, grad_kernel, attended,
+    field, cot, taps, time_weight, gain, w_query, w_key, w_value, w_out,
     col_out, cor_out, row_in, col_in, cor_in,
     pad_act, pad_cot, win_act, win_cot,
     grads, core_in, core_sum, x_in, y_out, y_in, z_out, z_in,
     q_buf, kv_buf, part_out, part_in,
-    halo_s, halo_r, group_s, group_r,
+    halo_s, halo_r, group_s, group_r, load_s,
 ):
+    loads = [
+        pltpu.make_async_copy(src, dst, load_s.at[i])
+        for i, (src, dst) in enumerate((
+            (field_hbm, field),
+            (cot_hbm, cot),
+            (time_weight_hbm, time_weight),
+            (taps_hbm, taps),
+            (gain_hbm, gain),
+            (w_query_hbm, w_query),
+            (w_key_hbm, w_key),
+            (w_value_hbm, w_value),
+            (w_out_hbm, w_out),
+        ))
+    ]
     lat, lon = lax.axis_index("lat"), lax.axis_index("lon")
     y, x, core = lat // 8, (lon // 2) % 4, lon % 2
     z = (lon // 8) * 8 + lat % 8
@@ -114,6 +132,11 @@
     everyone = near + [plane(k, 1) for k in range(NPLANE)] + [ring(d) for d in range(1, NZ)]
     for dev in everyone:
         pl.semaphore_signal(barrier, inc=1, device_id=dev, device_id_type=MESH)
+    for load in loads:
+        load.start()
+
+    for load in loads[0:2]:
+        load.wait()
 
     cell = lax.broadcasted_iota(jnp.int32, (32, CELLS), 1)
     line = lax.broadcasted_iota(jnp.int32, (32, CELLS), 0)
@@ -159,6 +182,8 @@
     xf = flat_field.astype(F32)
     pad_act[1 : ROWS + 1, 8 : 8 + COLS, :] = silu_rounded(xf).reshape(ROWS, COLS, C)
     pad_cot[1 : ROWS + 1, 8 : 8 + COLS, :] = flat_cot.astype(F32).reshape(ROWS, COLS, C)
+    for load in loads[2:]:
+        load.wait()
     tbias = embed_bias(step_ref[0], time_weight[...])
     row = lax.broadcasted_iota(jnp.int32, (C, C), 0)
     col = lax.broadcasted_iota(jnp.int32, (C, C), 1)
@@ -197,6 +222,11 @@
     def window(ref, a, b):
         return ref[b, a : a + ROWS].reshape(CELLS, C)
 
+    for tap in range(9):
+        part = dot(cot_t, window(win_act, tap // 3, tap % 3)).astype(BF16)
+        grads[:, :, tap] = part.reshape(2, 4, 32, C)
+    send(grads.at[1 - core], core_in, group_s.at[2], group_r.at[2], other)
+
     conv = xf + tbias
     for tap in range(9):
         conv = conv + dot(window(win_act, tap // 3, tap % 3), taps[tap])
@@ -215,15 +245,16 @@
     values = dot(normed, w_value[...])
     q_buf[NPLANE] = jnp.concatenate([query[:, 0:128], query[:, 128:256]], axis=0).astype(BF16)
     kv_buf[NRING] = jnp.concatenate([keys, values], axis=0).astype(BF16)
-    for d in range(1, NZ):
+    for d in RING:
         send(kv_buf.at[NRING], kv_buf.at[d - 1], group_s.at[0], group_r.at[0], ring(d))
     for k in range(NPLANE):
         send(q_buf.at[NPLANE], q_buf.at[k], group_s.at[1], group_r.at[1], plane(k, 1))
 
-    for tap in range(9):
-        part = dot(cot_t, window(win_act, tap // 3, tap % 3)).astype(BF16)
-        grads[:, :, tap] = part.reshape(2, 4, 32, C)
-    send(grads.at[1 - core], core_in, group_s.at[2], group_r.at[2], other)
+    await_recv(core_in, group_s.at[2], group_r.at[2], other)
+    core_sum[...] = (grads[core].astype(F32) + core_in[...].astype(F32)).astype(BF16)
+    for k in range(1, NX):
+        to = (x + k) % NX
+        send(core_sum.at[to], x_in.at[k - 1], group_s.at[3], group_r.at[3], device(y, z, to, core))
 
     for b in range(3):
         win_cot[b] = pad_cot[:, 7 + b : 7 + b + COLS, :].astype(BF16)
@@ -235,11 +266,21 @@
         (flat_cot.astype(F32) + back * sig * (1.0 + xf * (1.0 - sig))).astype(BF16).reshape(ROWS, COLS, C)
     )
 
-    await_recv(core_in, group_s.at[2], group_r.at[2], other)
-    core_sum[...] = (grads[core].astype(F32) + core_in[...].astype(F32)).astype(BF16)
-    for k in range(1, NX):
-        to = (x + k) % NX
-        send(core_sum.at[to], x_in.at[k - 1], group_s.at[3], group_r.at[3], device(y, z, to, core))
+    await_recv(x_in, group_s.at[3], group_r.at[3], other)
+    acc = core_sum[x].astype(F32)
+    for k in range(NX - 1):
+        acc = acc + x_in[k].astype(F32)
+    lane = lax.broadcasted_iota(jnp.int32, (9 * 16, 128), 1)
+    for t in range(2):
+        low = acc[:, 0:16, 128 * t : 128 * t + 128].reshape(9 * 16, 128)
+        high = acc[:, 16:32, 128 * t : 128 * t + 128].reshape(9 * 16, 128)
+        even = jnp.where(lane < 64, low, pltpu.roll(high, 64, 1))
+        odd = jnp.where(lane < 64, pltpu.roll(low, 64, 1), high)
+        y_out[2 * t] = even.astype(BF16)
+        y_out[2 * t + 1] = odd.astype(BF16)
+    for k in range(1, NY):
+        to = (y + k) % NY
+        send(y_out.at[to], y_in.at[k - 1], group_s.at[5], group_r.at[5], device(to, z, x, core))
 
     await_recv(kv_buf.at[0:NRING], group_s.at[0], group_r.at[0], other)
     await_recv(q_buf.at[0:NPLANE], group_s.at[1], group_r.at[1], other)
@@ -270,29 +311,13 @@
     for k in range(NPLANE):
         send(part_out.at[k], part_in.at[k], group_s.at[4], group_r.at[4], plane(k, -1))
 
-    await_recv(x_in, group_s.at[3], group_r.at[3], other)
-    acc = core_sum[x].astype(F32)
-    for k in range(NX - 1):
-        acc = acc + x_in[k].astype(F32)
-    lane = lax.broadcasted_iota(jnp.int32, (9 * 16, 128), 1)
-    for t in range(2):
-        low = acc[:, 0:16, 128 * t : 128 * t + 128].reshape(9 * 16, 128)
-        high = acc[:, 16:32, 128 * t : 128 * t + 128].reshape(9 * 16, 128)
-        even = jnp.where(lane < 64, low, pltpu.roll(high, 64, 1))
-        odd = jnp.where(lane < 64, pltpu.roll(low, 64, 1), high)
-        y_out[2 * t] = even.astype(BF16)
-        y_out[2 * t + 1] = odd.astype(BF16)
-    for k in range(1, NY):
-        to = (y + k) % NY
-        send(y_out.at[to], y_in.at[k - 1], group_s.at[5], group_r.at[5], device(to, z, x, core))
-
     await_recv(y_in, group_s.at[5], group_r.at[5], other)
     acc = y_out[y].astype(F32)
     for k in range(NY - 1):
         acc = acc + y_in[k].astype(F32)
     acc = jnp.concatenate([acc, jnp.zeros((256 - 144, 128), F32)], axis=0)
     z_out[...] = acc.T.reshape(NZ, 8, 256)
-    for d in range(1, NZ):
+    for d in RING:
         send(z_out.at[(z + d) % NZ], z_in.at[d - 1], group_s.at[6], group_r.at[6], ring(d))
 
     await_recv(part_in, group_s.at[4], group_r.at[4], other)
@@ -314,7 +339,9 @@
         weight = jnp.where(lane_q < 64, first, second).reshape(NPLANE + 1, 8, 128)
         halves.append(jnp.sum(part * weight, axis=0))
     mixed = jnp.concatenate(halves, axis=1).astype(BF16)
-    attended[...] = (pooled + dot(mixed, w_out[...])).astype(BF16)
+    result = pooled + dot(mixed, w_out[...])
+    attended[0] = result[0:4].astype(BF16)
+    attended[1] = result[4:8].astype(BF16)
 
     await_recv(z_in, group_s.at[6], group_r.at[6], other)
     acc = z_out[z]
@@ -329,21 +356,52 @@
         await_send(buf, group_s.at[i], group_r.at[i], other)
 
 
+OUTS = (
+    jax.ShapeDtypeStruct((ROWS, COLS, C), BF16),
+    jax.ShapeDtypeStruct((ROWS, COLS, C), BF16),
+    jax.ShapeDtypeStruct((9, 8, 16), F32),
+    jax.ShapeDtypeStruct((ROWS // POOL, COLS // POOL, C), BF16),
+)
+
+
+def finish_body(*refs):
+    stores = [pltpu.make_async_copy(refs[i], refs[4 + i], refs[8].at[i]) for i in range(4)]
+    for store in stores:
+        store.start()
+    for store in stores:
+        store.wait()
+
+
+def finish(results):
+    return pl.pallas_call(
+        finish_body,
+        out_shape=OUTS,
+        in_specs=[pl.BlockSpec(memory_space=pltpu.VMEM)] * 4,
+        out_specs=(pl.BlockSpec(memory_space=pltpu.HBM),) * 4,
+        scratch_shapes=[pltpu.SemaphoreType.DMA((4,))],
+        compiler_params=pltpu.CompilerParams(vmem_limit_bytes=8 * 1024 * 1024),
+    )(*results)
+
+
 def shards(
     field, cotangent, kernel, timestep, time_weight, norm_gain, w_query, w_key, w_value, w_out
 ):
-    vmem = pl.BlockSpec(memory_space=pltpu.VMEM)
+    hbm = pl.BlockSpec(memory_space=pltpu.HBM)
     call = pl.pallas_call(
         body,
-        out_shape=(
-            jax.ShapeDtypeStruct((ROWS, COLS, C), BF16),
-            jax.ShapeDtypeStruct((ROWS, COLS, C), BF16),
-            jax.ShapeDtypeStruct((9, 8, 16), F32),
-            jax.ShapeDtypeStruct((8, C), BF16),
-        ),
-        in_specs=[pl.BlockSpec(memory_space=pltpu.SMEM)] + [vmem] * 9,
-        out_specs=(vmem,) * 4,
+        out_shape=OUTS,
+        in_specs=[pl.BlockSpec(memory_space=pltpu.SMEM)] + [hbm] * 9,
+        out_specs=(pl.BlockSpec(memory_space=pltpu.VMEM),) * 4,
         scratch_shapes=[
+            pltpu.VMEM((ROWS, COLS, C), BF16),
+            pltpu.VMEM((ROWS, COLS, C), BF16),
+            pltpu.VMEM((9, C, C), BF16),
+            pltpu.VMEM((TE, C), F32),
+            pltpu.VMEM((1, C), F32),
+            pltpu.VMEM((C, C), BF16),
+            pltpu.VMEM((C, C), BF16),
+            pltpu.VMEM((C, C), BF16),
+            pltpu.VMEM((C, C), BF16),
             pltpu.VMEM((2, 32, C), BF16),
             pltpu.VMEM((4, 8, C), F32),
             pltpu.VMEM((2, 2, COLS, C), BF16),
@@ -369,16 +427,17 @@
             pltpu.SemaphoreType.DMA((10,)),
             pltpu.SemaphoreType.DMA((7,)),
             pltpu.SemaphoreType.DMA((7,)),
+            pltpu.SemaphoreType.DMA((9,)),
         ],
         compiler_params=pltpu.CompilerParams(
-            collective_id=0, has_side_effects=True, vmem_limit_bytes=48 * 1024 * 1024
+            collective_id=0, has_side_effects=True, vmem_limit_bytes=40 * 1024 * 1024
         ),
     )
-    block_out, grad_field, grad_kernel, attended = call(
-        timestep, field, cotangent, kernel, time_weight, norm_gain.reshape(1, C),
-        w_query, w_key, w_value, w_out,
+    operands = (
+        field, cotangent, kernel, time_weight, norm_gain.reshape(1, C), w_query, w_key, w_value, w_out
     )
-    return block_out, grad_field, grad_kernel, attended.reshape(ROWS // POOL, COLS // POOL, C)
+    results = call(timestep, *(pltpu.with_memory_space_constraint(v, pltpu.HBM) for v in operands))
+    return finish(results)
 
 
 def solution(mesh):

time: 70.9 us -> 55.8 us (0.79)
  local copies, waits for them, and re-layouts: 11 us -> 0 us
  Pallas kernels: 58.2 us -> 54.4 us
    unnamed x21 -> x0, local copies, waits for them, and re-layouts: 10.4 us -> none
    pallas_call x1 -> x2, Pallas kernels: 58.2 us -> 54.4 us  [the longest x1 53.5 us: shards(): call(timestep, *(pltpu.with_memory_space_constraint(v, pltpu.HBM) for v i...]
where the time goes in v2:
time: 55.8 us; the launch traced here: 55.7 us
  Pallas kernels  54.4 us (97%)
  between operations  1.29 us (2%)
    pallas_call x1, Pallas kernels, shards(): call(timestep, *(pltpu.with_memory_space_constraint(v, pltpu.HBM) for v i...  53.5 us

profile of v2, /device:TPU:4, one launch (start us, length us, event | category | flops | bytes accessed | tf_op | source)
XLA Modules:
  0.0 55.7 jit_solution(8278002459562623256)
XLA Ops:
  1.3 53.5 %shard_map.129 = (bf16[16,32,256]{2,1,0:T(8,128)(2,1)S(1)}, bf16[16,32,256]{2,1,0:T(8,128)(2,1)S(1)}, f32[9,8,16]{2,1,0:T(8,128)S(1)}, bf16[2,4,256]{2,1,0:T(4,128)(2,1)S(1)}) custom-call(s32[1]{0:T(128)S(6)} %copy.14.step_ref, bf16[16,32,256]{2,1,0:T(8,128)(2,1)} %field_hbm.1, bf16[16,32,256]{2,1,0:T(8,128)(2,1)} %cot_hbm.1, bf16[9,256,256]{2,1,0:T(8,128)(2,1)} %taps_hbm.1, ...), custom_call_target="tpu_custom_call" | custom-call | tf_op jit(solution)/shard_map/pallas_call | solution.py:439
  54.8 0.8 %shard_map.130 = (bf16[16,32,256]{2,1,0:T(8,128)(2,1)}, bf16[16,32,256]{2,1,0:T(8,128)(2,1)}, f32[9,8,16]{2,1,0:T(8,128)}, bf16[2,4,256]{2,1,0:T(4,128)(2,1)}) custom-call(bf16[16,32,256]{2,1,0:T(8,128)(2,1)S(1)} %get-tuple-element.8.refs_0_, bf16[16,32,256]{2,1,0:T(8,128)(2,1)S(1)} %get-tuple-element.9.refs_1_, f32[9,8,16]{2,1,0:T(8,128)S(1)} %get-tuple-element.10.refs_2_, ...), custom_call_target="tpu_custom_call" | custom-call | tf_op jit(solution)/shard_map/pallas_call | solution.py:376

commit v3 on v2

--- a/solution.py
+++ b/solution.py
@@ -18,6 +18,7 @@
 NY, NZ, NX, NC = 4, 16, 4, 2
 ROWS, COLS, C = 16, 32, 256
 CELLS = ROWS * COLS
+TAPS_P = 5
 PLANE = [
     (dy, dx, dc) for dy in range(NY) for dx in range(NX) for dc in range(NC) if (dy, dx, dc) != (0, 0, 0)
 ]
@@ -76,6 +77,18 @@
     ).wait_send()
 
 
+def by_y(cells):
+    rows = 16 * cells.shape[0]
+    lane = lax.broadcasted_iota(jnp.int32, (rows, 128), 1)
+    blocks = []
+    for t in range(2):
+        low = cells[:, 0:16, 128 * t : 128 * t + 128].reshape(rows, 128)
+        high = cells[:, 16:32, 128 * t : 128 * t + 128].reshape(rows, 128)
+        blocks.append(jnp.where(lane < 64, low, pltpu.roll(high, 64, 1)))
+        blocks.append(jnp.where(lane < 64, pltpu.roll(low, 64, 1), high))
+    return blocks
+
+
 def embed_bias(step, time_weight):
     half = TE // 2
     index = lax.broadcasted_iota(jnp.int32, (8, half), 1).astype(F32)
@@ -93,7 +106,8 @@
     field, cot, taps, time_weight, gain, w_query, w_key, w_value, w_out,
     col_out, cor_out, row_in, col_in, cor_in,
     pad_act, pad_cot, win_act, win_cot,
-    grads, core_in, core_sum, x_in, y_out, y_in, z_out, z_in,
+    grads_p, core_in_p, x_out_p, x_in_p, y_out_p, y_in_p,
+    grads_q, core_in_q, y_out_q, y_in_q, x_out_q, x_in_q, z_out, z_in,
     q_buf, kv_buf, part_out, part_in,
     halo_s, halo_r, group_s, group_r, load_s,
 ):
@@ -223,9 +237,14 @@
         return ref[b, a : a + ROWS].reshape(CELLS, C)
 
     for tap in range(9):
-        part = dot(cot_t, window(win_act, tap // 3, tap % 3)).astype(BF16)
-        grads[:, :, tap] = part.reshape(2, 4, 32, C)
-    send(grads.at[1 - core], core_in, group_s.at[2], group_r.at[2], other)
+        part = dot(cot_t, window(win_act, tap // 3, tap % 3)).astype(BF16).reshape(2, 4, 32, C)
+        if tap < TAPS_P:
+            grads_p[:, :, tap] = part
+        else:
+            grads_q[:, :, tap - TAPS_P] = part
+        if tap == TAPS_P - 1:
+            send(grads_p.at[1 - core], core_in_p, group_s.at[2], group_r.at[2], other)
+    send(grads_q.at[1 - core], core_in_q, group_s.at[7], group_r.at[7], other)
 
     conv = xf + tbias
     for tap in range(9):
@@ -247,14 +266,21 @@
     kv_buf[NRING] = jnp.concatenate([keys, values], axis=0).astype(BF16)
     for d in RING:
         send(kv_buf.at[NRING], kv_buf.at[d - 1], group_s.at[0], group_r.at[0], ring(d))
+
+    await_recv(core_in_p, group_s.at[2], group_r.at[2], other)
+    x_out_p[...] = (grads_p[core].astype(F32) + core_in_p[...].astype(F32)).astype(BF16)
+    for k in (2, 1, 3):
+        to = (x + k) % NX
+        send(x_out_p.at[to], x_in_p.at[k - 1], group_s.at[3], group_r.at[3], device(y, z, to, core))
+    await_recv(core_in_q, group_s.at[7], group_r.at[7], other)
+    acc = grads_q[core].astype(F32) + core_in_q[...].astype(F32)
+    for i, block in enumerate(by_y(acc.reshape(4 * (9 - TAPS_P), 32, C))):
+        y_out_q[i] = block.astype(BF16)
+    for k in (2, 1, 3):
+        to = (y + k) % NY
+        send(y_out_q.at[to], y_in_q.at[k - 1], group_s.at[8], group_r.at[8], device(to, z, x, core))
     for k in range(NPLANE):
         send(q_buf.at[NPLANE], q_buf.at[k], group_s.at[1], group_r.at[1], plane(k, 1))
-
-    await_recv(core_in, group_s.at[2], group_r.at[2], other)
-    core_sum[...] = (grads[core].astype(F32) + core_in[...].astype(F32)).astype(BF16)
-    for k in range(1, NX):
-        to = (x + k) % NX
-        send(core_sum.at[to], x_in.at[k - 1], group_s.at[3], group_r.at[3], device(y, z, to, core))
 
     for b in range(3):
         win_cot[b] = pad_cot[:, 7 + b : 7 + b + COLS, :].astype(BF16)
@@ -266,21 +292,23 @@
         (flat_cot.astype(F32) + back * sig * (1.0 + xf * (1.0 - sig))).astype(BF16).reshape(ROWS, COLS, C)
     )
 
-    await_recv(x_in, group_s.at[3], group_r.at[3], other)
-    acc = core_sum[x].astype(F32)
+    await_recv(x_in_p, group_s.at[3], group_r.at[3], other)
+    acc = x_out_p[x].astype(F32)
     for k in range(NX - 1):
-        acc = acc + x_in[k].astype(F32)
-    lane = lax.broadcasted_iota(jnp.int32, (9 * 16, 128), 1)
-    for t in range(2):
-        low = acc[:, 0:16, 128 * t : 128 * t + 128].reshape(9 * 16, 128)
-        high = acc[:, 16:32, 128 * t : 128 * t + 128].reshape(9 * 16, 128)
-        even = jnp.where(lane < 64, low, pltpu.roll(high, 64, 1))
-        odd = jnp.where(lane < 64, pltpu.roll(low, 64, 1), high)
-        y_out[2 * t] = even.astype(BF16)
-        y_out[2 * t + 1] = odd.astype(BF16)
-    for k in range(1, NY):
+        acc = acc + x_in_p[k].astype(F32)
+    for i, block in enumerate(by_y(acc)):
+        y_out_p[i] = block.astype(BF16)
+    for k in (2, 1, 3):
         to = (y + k) % NY
-        send(y_out.at[to], y_in.at[k - 1], group_s.at[5], group_r.at[5], device(to, z, x, core))
+        send(y_out_p.at[to], y_in_p.at[k - 1], group_s.at[5], group_r.at[5], device(to, z, x, core))
+    await_recv(y_in_q, group_s.at[8], group_r.at[8], other)
+    acc = y_out_q[y].astype(F32)
+    for k in range(NY - 1):
+        acc = acc + y_in_q[k].astype(F32)
+    x_out_q[...] = acc.astype(BF16).reshape(x_out_q.shape)
+    for k in (2, 1, 3):
+        to = (x + k) % NX
+        send(x_out_q.at[to], x_in_q.at[k - 1], group_s.at[9], group_r.at[9], device(y, z, to, core))
 
     await_recv(kv_buf.at[0:NRING], group_s.at[0], group_r.at[0], other)
     await_recv(q_buf.at[0:NPLANE], group_s.at[1], group_r.at[1], other)
@@ -311,12 +339,15 @@
     for k in range(NPLANE):
         send(part_out.at[k], part_in.at[k], group_s.at[4], group_r.at[4], plane(k, -1))
 
-    await_recv(y_in, group_s.at[5], group_r.at[5], other)
-    acc = y_out[y].astype(F32)
+    await_recv(y_in_p, group_s.at[5], group_r.at[5], other)
+    await_recv(x_in_q, group_s.at[9], group_r.at[9], other)
+    acc_p = y_out_p[y].astype(F32)
+    acc_q = x_out_q[x].astype(F32)
     for k in range(NY - 1):
-        acc = acc + y_in[k].astype(F32)
-    acc = jnp.concatenate([acc, jnp.zeros((256 - 144, 128), F32)], axis=0)
-    z_out[...] = acc.T.reshape(NZ, 8, 256)
+        acc_p = acc_p + y_in_p[k].astype(F32)
+        acc_q = acc_q + x_in_q[k].astype(F32)
+    acc = jnp.concatenate([acc_p, acc_q, jnp.zeros((256 - 144, 128), F32)], axis=0).T.reshape(NZ, 8, 256)
+    z_out[...] = jnp.concatenate([acc[:, :, 0:128], acc[:, :, 128:256]], axis=1).astype(BF16)
     for d in RING:
         send(z_out.at[(z + d) % NZ], z_in.at[d - 1], group_s.at[6], group_r.at[6], ring(d))
 
@@ -344,15 +375,18 @@
     attended[1] = result[4:8].astype(BF16)
 
     await_recv(z_in, group_s.at[6], group_r.at[6], other)
-    acc = z_out[z]
+    acc = z_out[z].astype(F32)
     for k in range(NRING):
-        acc = acc + z_in[k]
-    for tap in range(9):
-        grad_kernel[tap] = acc[:, 16 * tap : 16 * tap + 16]
+        acc = acc + z_in[k].astype(F32)
+    for tap in range(8):
+        grad_kernel[tap] = acc[0:8, 16 * tap : 16 * tap + 16]
+    grad_kernel[8] = acc[8:16, 0:16]
 
     for copy in copies:
         copy.wait_send()
-    for i, buf in enumerate((kv_buf.at[0:NRING], q_buf.at[0:NPLANE], core_in, x_in, part_in, y_in, z_in)):
+    for i, buf in enumerate((
+        kv_buf.at[0:NRING], q_buf.at[0:NPLANE], core_in_p, x_in_p, part_in, y_in_p, z_in, core_in_q, y_in_q, x_in_q
+    )):
         await_send(buf, group_s.at[i], group_r.at[i], other)
 
 
@@ -411,22 +445,28 @@
             pltpu.VMEM((ROWS + 2, COLS + 16, C), F32),
             pltpu.VMEM((3, ROWS + 2, COLS, C), BF16),
             pltpu.VMEM((3, ROWS + 2, COLS, C), BF16),
-            pltpu.VMEM((2, 4, 9, 32, C), BF16),
-            pltpu.VMEM((4, 9, 32, C), BF16),
-            pltpu.VMEM((4, 9, 32, C), BF16),
-            pltpu.VMEM((NX - 1, 9, 32, C), BF16),
-            pltpu.VMEM((NY, 144, 128), BF16),
-            pltpu.VMEM((NY - 1, 144, 128), BF16),
-            pltpu.VMEM((NZ, 8, 256), F32),
-            pltpu.VMEM((NRING, 8, 256), F32),
+            pltpu.VMEM((2, 4, TAPS_P, 32, C), BF16),
+            pltpu.VMEM((4, TAPS_P, 32, C), BF16),
+            pltpu.VMEM((4, TAPS_P, 32, C), BF16),
+            pltpu.VMEM((NX - 1, TAPS_P, 32, C), BF16),
+            pltpu.VMEM((NY, TAPS_P * 16, 128), BF16),
+            pltpu.VMEM((NY - 1, TAPS_P * 16, 128), BF16),
+            pltpu.VMEM((2, 4, 9 - TAPS_P, 32, C), BF16),
+            pltpu.VMEM((4, 9 - TAPS_P, 32, C), BF16),
+            pltpu.VMEM((NY, 4 * (9 - TAPS_P) * 16, 128), BF16),
+            pltpu.VMEM((NY - 1, 4 * (9 - TAPS_P) * 16, 128), BF16),
+            pltpu.VMEM((NX, (9 - TAPS_P) * 16, 128), BF16),
+            pltpu.VMEM((NX - 1, (9 - TAPS_P) * 16, 128), BF16),
+            pltpu.VMEM((NZ, 16, 128), BF16),
+            pltpu.VMEM((NRING, 16, 128), BF16),
             pltpu.VMEM((NPLANE + 1, 16, 128), BF16),
             pltpu.VMEM((NZ, 16, C), BF16),
             pltpu.VMEM((NPLANE + 1, 8, 384), F32),
             pltpu.VMEM((NPLANE, 8, 384), F32),
             pltpu.SemaphoreType.DMA((10,)),
             pltpu.SemaphoreType.DMA((10,)),
-            pltpu.SemaphoreType.DMA((7,)),
-            pltpu.SemaphoreType.DMA((7,)),
+            pltpu.SemaphoreType.DMA((10,)),
+            pltpu.SemaphoreType.DMA((10,)),
             pltpu.SemaphoreType.DMA((9,)),
         ],
         compiler_params=pltpu.CompilerParams(

time: 55.8 us -> 49.2 us (0.88)
  the two profiles are of different devices: /device:TPU:4 before, /device:TPU:1 now
where the time goes in v3:
time: 49.2 us; the launch traced here: 49 us
  Pallas kernels  47.8 us (97%)
  between operations  1.29 us (3%)
    pallas_call x1, Pallas kernels, shards(): call(timestep, *(pltpu.with_memory_space_constraint(v, pltpu.HBM) for v i...  46.9 us

profile of v3, /device:TPU:1, one launch (start us, length us, event | category | flops | bytes accessed | tf_op | source)
XLA Modules:
  0.0 49.0 jit_solution(11514340382869520853)
XLA Ops:
  1.3 46.9 %shard_map.129 = (bf16[16,32,256]{2,1,0:T(8,128)(2,1)S(1)}, bf16[16,32,256]{2,1,0:T(8,128)(2,1)S(1)}, f32[9,8,16]{2,1,0:T(8,128)S(1)}, bf16[2,4,256]{2,1,0:T(4,128)(2,1)S(1)}) custom-call(s32[1]{0:T(128)S(6)} %copy.14.step_ref, bf16[16,32,256]{2,1,0:T(8,128)(2,1)} %field_hbm.1, bf16[16,32,256]{2,1,0:T(8,128)(2,1)} %cot_hbm.1, bf16[9,256,256]{2,1,0:T(8,128)(2,1)} %taps_hbm.1, ...), custom_call_target="tpu_custom_call" | custom-call | tf_op jit(solution)/shard_map/pallas_call | solution.py:479
  48.2 0.8 %shard_map.130 = (bf16[16,32,256]{2,1,0:T(8,128)(2,1)}, bf16[16,32,256]{2,1,0:T(8,128)(2,1)}, f32[9,8,16]{2,1,0:T(8,128)}, bf16[2,4,256]{2,1,0:T(4,128)(2,1)}) custom-call(bf16[16,32,256]{2,1,0:T(8,128)(2,1)S(1)} %get-tuple-element.8.refs_0_, bf16[16,32,256]{2,1,0:T(8,128)(2,1)S(1)} %get-tuple-element.9.refs_1_, f32[9,8,16]{2,1,0:T(8,128)S(1)} %get-tuple-element.10.refs_2_, ...), custom_call_target="tpu_custom_call" | custom-call | tf_op jit(solution)/shard_map/pallas_call | solution.py:410

commit v4 on v3

--- a/solution.py
+++ b/solution.py
@@ -22,9 +22,14 @@
 PLANE = [
     (dy, dx, dc) for dy in range(NY) for dx in range(NX) for dc in range(NC) if (dy, dx, dc) != (0, 0, 0)
 ]
-PLANE.sort(key=lambda d: -(min(d[0], NY - d[0]) + min(d[1], NX - d[1]) + 0.5 * d[2]))
+PLANE.sort(key=lambda d: (-d[2], -(min(d[0], NY - d[0]) + min(d[1], NX - d[1]))))
 NPLANE = len(PLANE)
+SPREAD = sorted(
+    range(NPLANE), key=lambda k: -(min(PLANE[k][0], NY - PLANE[k][0]) + min(PLANE[k][1], NX - PLANE[k][1]))
+)
 RING = sorted(range(1, NZ), key=lambda d: -min(d, NZ - d))
+LINE = [(dz, dc) for dz in RING + [0] for dc in range(NC) if (dz, dc) != (0, 0)]
+NLINE = len(LINE)
 NRING = NZ - 1
 
 
@@ -108,7 +113,7 @@
     pad_act, pad_cot, win_act, win_cot,
     grads_p, core_in_p, x_out_p, x_in_p, y_out_p, y_in_p,
     grads_q, core_in_q, y_out_q, y_in_q, x_out_q, x_in_q, z_out, z_in,
-    q_buf, kv_buf, part_out, part_in,
+    q_buf, kv_out, kv_buf, part_out, part_in,
     halo_s, halo_r, group_s, group_r, load_s,
 ):
     loads = [
@@ -133,8 +138,8 @@
         dy, dx, dc = PLANE[k]
         return device((y + sign * dy + NY) % NY, z, (x + sign * dx + NX) % NX, (core + dc) % NC)
 
-    def ring(dz):
-        return device(y, (z + dz + NZ) % NZ, x, core)
+    def ring(dz, dc=0):
+        return device(y, (z + dz + NZ) % NZ, x, (core + dc) % NC)
 
     up, down = (lat + 31) % 32, (lat + 1) % 32
     left, right = (lon + 15) % 16, (lon + 1) % 16
@@ -143,7 +148,7 @@
     other = (lat, lon + 1 - 2 * core)
 
     barrier = pltpu.get_barrier_semaphore()
-    everyone = near + [plane(k, 1) for k in range(NPLANE)] + [ring(d) for d in range(1, NZ)]
+    everyone = near + [plane(k, 1) for k in range(NPLANE)] + [ring(*d) for d in LINE]
     for dev in everyone:
         pl.semaphore_signal(barrier, inc=1, device_id=dev, device_id_type=MESH)
     for load in loads:
@@ -246,27 +251,6 @@
             send(grads_p.at[1 - core], core_in_p, group_s.at[2], group_r.at[2], other)
     send(grads_q.at[1 - core], core_in_q, group_s.at[7], group_r.at[7], other)
 
-    conv = xf + tbias
-    for tap in range(9):
-        conv = conv + dot(window(win_act, tap // 3, tap % 3), taps[tap])
-    rounded = conv.astype(BF16)
-    block_out[...] = rounded.reshape(ROWS, COLS, C)
-
-    token = lax.broadcasted_iota(jnp.int32, (8, CELLS), 0)
-    cell8 = lax.broadcasted_iota(jnp.int32, (8, CELLS), 1)
-    its_token = (cell8 // (COLS * POOL)) * 4 + (cell8 % COLS) // POOL
-    pooled = dot(jnp.where(token == its_token, 1.0, 0.0).astype(BF16), rounded) * (1.0 / (POOL * POOL))
-    center = pooled - jnp.mean(pooled, axis=1, keepdims=True)
-    spread = jnp.mean(center * center, axis=1, keepdims=True)
-    normed = (center * lax.rsqrt(spread + 1e-05) * gain[...]).astype(BF16)
-    query = dot(normed, w_query[...])
-    keys = dot(normed, w_key[...])
-    values = dot(normed, w_value[...])
-    q_buf[NPLANE] = jnp.concatenate([query[:, 0:128], query[:, 128:256]], axis=0).astype(BF16)
-    kv_buf[NRING] = jnp.concatenate([keys, values], axis=0).astype(BF16)
-    for d in RING:
-        send(kv_buf.at[NRING], kv_buf.at[d - 1], group_s.at[0], group_r.at[0], ring(d))
-
     await_recv(core_in_p, group_s.at[2], group_r.at[2], other)
     x_out_p[...] = (grads_p[core].astype(F32) + core_in_p[...].astype(F32)).astype(BF16)
     for k in (2, 1, 3):
@@ -279,7 +263,31 @@
     for k in (2, 1, 3):
         to = (y + k) % NY
         send(y_out_q.at[to], y_in_q.at[k - 1], group_s.at[8], group_r.at[8], device(to, z, x, core))
-    for k in range(NPLANE):
+
+    conv = xf + tbias
+    for tap in range(9):
+        conv = conv + dot(window(win_act, tap // 3, tap % 3), taps[tap])
+    rounded = conv.astype(BF16)
+    block_out[...] = rounded.reshape(ROWS, COLS, C)
+
+    token = lax.broadcasted_iota(jnp.int32, (8, CELLS), 0)
+    cell8 = lax.broadcasted_iota(jnp.int32, (8, CELLS), 1)
+    its_token = (cell8 // (COLS * POOL)) * 4 + (cell8 % COLS) // POOL
+    pooled = dot(jnp.where(token == its_token, 1.0, 0.0).astype(BF16), rounded) * (1.0 / (POOL * POOL))
+    center = pooled - jnp.mean(pooled, axis=1, keepdims=True)
+    spread = jnp.mean(center * center, axis=1, keepdims=True)
+    normed = (center * lax.rsqrt(spread + 1e-05) * gain[...]).astype(BF16)
+    query = dot(normed, w_query[...])
+    keys = dot(normed, w_key[...])
+    values = dot(normed, w_value[...])
+    q_buf[NPLANE] = jnp.concatenate([query[:, 0:128], query[:, 128:256]], axis=0).astype(BF16)
+    for pair in range(2):
+        part = slice(128 * pair, 128 * pair + 128)
+        kv_out[pair] = jnp.concatenate([keys[:, part], values[:, part]], axis=0).astype(BF16)
+    kv_buf[NLINE] = kv_out[core]
+    for k, d in enumerate(LINE):
+        send(kv_out.at[(core + d[1]) % NC], kv_buf.at[k], group_s.at[0], group_r.at[0], ring(*d))
+    for k in SPREAD:
         send(q_buf.at[NPLANE], q_buf.at[k], group_s.at[1], group_r.at[1], plane(k, 1))
 
     for b in range(3):
@@ -310,35 +318,6 @@
         to = (x + k) % NX
         send(x_out_q.at[to], x_in_q.at[k - 1], group_s.at[9], group_r.at[9], device(y, z, to, core))
 
-    await_recv(kv_buf.at[0:NRING], group_s.at[0], group_r.at[0], other)
-    await_recv(q_buf.at[0:NPLANE], group_s.at[1], group_r.at[1], other)
-    nq, nk = 8 * (NPLANE + 1), 8 * NZ
-    q32 = q_buf[...].astype(F32)
-    kv32 = kv_buf[...].astype(F32)
-    all_k = kv32[:, 0:8, :].reshape(nk, C).astype(BF16)
-    all_v = kv32[:, 8:16, :].reshape(nk, C).astype(BF16)
-    lane_q = lax.broadcasted_iota(jnp.int32, (nq, 128), 1)
-    lane_k = lax.broadcasted_iota(jnp.int32, (nk, 128), 1)
-    lse = jnp.zeros((nq, 128), F32)
-    for pair in range(2):
-        q2 = q32[:, 8 * pair : 8 * pair + 8, :].reshape(nq, 128)
-        k2 = all_k[:, 128 * pair : 128 * pair + 128]
-        v2 = all_v[:, 128 * pair : 128 * pair + 128].astype(F32)
-        mixed2 = jnp.zeros((nq, 128), F32)
-        for h in range(2):
-            qm = jnp.where(lane_q // HEAD_DIM == h, q2, 0.0).astype(BF16)
-            vm = jnp.where(lane_k // HEAD_DIM == h, v2, 0.0).astype(BF16)
-            scores = dot_t(qm, k2) * (1.0 / math.sqrt(HEAD_DIM))
-            top = jnp.max(scores, axis=1, keepdims=True)
-            probs = jnp.exp(scores - top)
-            total = jnp.sum(probs, axis=1, keepdims=True)
-            mixed2 = mixed2 + dot(probs.astype(BF16), vm) * (1.0 / total)
-            lse = jnp.where(lane_q // 32 == 2 * pair + h, top + jnp.log(total), lse)
-        part_out[:, :, 128 * pair : 128 * pair + 128] = mixed2.reshape(NPLANE + 1, 8, 128)
-    part_out[:, :, 256:384] = lse.reshape(NPLANE + 1, 8, 128)
-    for k in range(NPLANE):
-        send(part_out.at[k], part_in.at[k], group_s.at[4], group_r.at[4], plane(k, -1))
-
     await_recv(y_in_p, group_s.at[5], group_r.at[5], other)
     await_recv(x_in_q, group_s.at[9], group_r.at[9], other)
     acc_p = y_out_p[y].astype(F32)
@@ -351,25 +330,59 @@
     for d in RING:
         send(z_out.at[(z + d) % NZ], z_in.at[d - 1], group_s.at[6], group_r.at[6], ring(d))
 
+    await_recv(kv_buf.at[0:NLINE], group_s.at[0], group_r.at[0], other)
+    await_recv(q_buf.at[0:NPLANE], group_s.at[1], group_r.at[1], other)
+    nq, nk = 8 * (NPLANE + 1), 8 * (NLINE + 1)
+    q32 = q_buf[...].astype(F32)
+    q2 = jnp.where(core == 0, q32[:, 0:8, :], q32[:, 8:16, :]).reshape(nq, 128)
+    kv32 = kv_buf[...].astype(F32)
+    k2 = kv32[:, 0:8, :].reshape(nk, 128).astype(BF16)
+    v2 = kv32[:, 8:16, :].reshape(nk, 128)
+    lane_q = lax.broadcasted_iota(jnp.int32, (nq, 128), 1)
+    lane_k = lax.broadcasted_iota(jnp.int32, (nk, 128), 1)
+    mixed2 = jnp.zeros((nq, 128), F32)
+    lse = []
+    for h in range(2):
+        qm = jnp.where(lane_q // HEAD_DIM == h, q2, 0.0).astype(BF16)
+        vm = jnp.where(lane_k // HEAD_DIM == h, v2, 0.0).astype(BF16)
+        scores = dot_t(qm, k2) * (1.0 / math.sqrt(HEAD_DIM))
+        top = jnp.max(scores, axis=1, keepdims=True)
+        probs = jnp.exp(scores - top)
+        total = jnp.sum(probs, axis=1, keepdims=True)
+        mixed2 = mixed2 + dot(probs.astype(BF16), vm) * (1.0 / total)
+        lse.append(top + jnp.log(total))
+    rest = jnp.where(lane_q < HEAD_DIM, lse[0], lse[1])
+    high = rest.astype(BF16).astype(F32)
+    rest = rest - high
+    middle = rest.astype(BF16).astype(F32)
+    place = (lane_q % HEAD_DIM) // 16
+    terms = jnp.where(place == 0, high, jnp.where(place == 1, middle, rest - middle))
+    part_out[...] = jnp.concatenate(
+        [mixed2.reshape(NPLANE + 1, 8, 128), terms.reshape(NPLANE + 1, 8, 128)], axis=1
+    ).astype(BF16)
+    for k in SPREAD:
+        send(part_out.at[k], part_in.at[k], group_s.at[4], group_r.at[4], plane(k, -1))
+
     await_recv(part_in, group_s.at[4], group_r.at[4], other)
-    lse = jnp.concatenate([part_in[:, :, 256:384], part_out[NPLANE:, :, 256:384]], axis=0)
-    top = jnp.max(lse, axis=0, keepdims=True)
-    share = jnp.exp(lse - top)
-    share = (share / jnp.sum(share, axis=0, keepdims=True)).reshape(nq, 128)
-    halves = []
-    for pair in range(2):
-        part = jnp.concatenate(
-            [
-                part_in[:, :, 128 * pair : 128 * pair + 128],
-                part_out[NPLANE:, :, 128 * pair : 128 * pair + 128],
-            ],
-            axis=0,
-        )
-        first = share[:, 64 * pair : 64 * pair + 1]
-        second = share[:, 64 * pair + 32 : 64 * pair + 33]
-        weight = jnp.where(lane_q < 64, first, second).reshape(NPLANE + 1, 8, 128)
-        halves.append(jnp.sum(part * weight, axis=0))
-    mixed = jnp.concatenate(halves, axis=1).astype(BF16)
+    parts = jnp.concatenate([part_in[...], part_out[NPLANE:]], axis=0).astype(F32)
+    half = (NPLANE + 1) // 2
+    lane_h = lax.broadcasted_iota(jnp.int32, (8 * half, 128), 1)
+    pairs = []
+    for g in range(2):
+        group = parts[g * half : g * half + half]
+        terms = group[:, 8:16, :].reshape(8 * half, 128)
+        sums = [
+            terms[:, c : c + 1] + terms[:, c + 16 : c + 17] + terms[:, c + 32 : c + 33]
+            for c in (0, HEAD_DIM)
+        ]
+        lse = jnp.where(lane_h < HEAD_DIM, sums[0], sums[1]).reshape(half, 8, 128)
+        share = jnp.exp(lse - jnp.max(lse, axis=0, keepdims=True))
+        share = share / jnp.sum(share, axis=0, keepdims=True)
+        pairs.append(jnp.sum(group[:, 0:8, :] * share, axis=0))
+    theirs, mine = pairs
+    mixed = jnp.concatenate(
+        [jnp.where(core == 0, mine, theirs), jnp.where(core == 0, theirs, mine)], axis=1
+    ).astype(BF16)
     result = pooled + dot(mixed, w_out[...])
     attended[0] = result[0:4].astype(BF16)
     attended[1] = result[4:8].astype(BF16)
@@ -385,7 +398,7 @@
     for copy in copies:
         copy.wait_send()
     for i, buf in enumerate((
-        kv_buf.at[0:NRING], q_buf.at[0:NPLANE], core_in_p, x_in_p, part_in, y_in_p, z_in, core_in_q, y_in_q, x_in_q
+        kv_buf.at[0:NLINE], q_buf.at[0:NPLANE], core_in_p, x_in_p, part_in, y_in_p, z_in, core_in_q, y_in_q, x_in_q
     )):
         await_send(buf, group_s.at[i], group_r.at[i], other)
 
@@ -460,9 +473,10 @@
             pltpu.VMEM((NZ, 16, 128), BF16),
             pltpu.VMEM((NRING, 16, 128), BF16),
             pltpu.VMEM((NPLANE + 1, 16, 128), BF16),
-            pltpu.VMEM((NZ, 16, C), BF16),
-            pltpu.VMEM((NPLANE + 1, 8, 384), F32),
-            pltpu.VMEM((NPLANE, 8, 384), F32),
+            pltpu.VMEM((2, 16, 128), BF16),
+            pltpu.VMEM((NLINE + 1, 16, 128), BF16),
+            pltpu.VMEM((NPLANE + 1, 16, 128), BF16),
+            pltpu.VMEM((NPLANE, 16, 128), BF16),
             pltpu.SemaphoreType.DMA((10,)),
             pltpu.SemaphoreType.DMA((10,)),
             pltpu.SemaphoreType.DMA((10,)),

time: 49.2 us -> 48.3 us (0.982)
  Pallas kernels: 47.8 us -> 46.8 us
    pallas_call x1, Pallas kernels: 46.9 us -> 46 us  [shards(): call(timestep, *(pltpu.with_memory_space_constraint(v, pltpu.HBM) for v i...]
where the time goes in v4:
time: 48.3 us; the launch traced here: 48.1 us
  Pallas kernels  46.8 us (97%)
  between operations  1.29 us (3%)
    pallas_call x1, Pallas kernels, shards(): call(timestep, *(pltpu.with_memory_space_constraint(v, pltpu.HBM) for v i...  46 us

profile of v4, /device:TPU:1, one launch (start us, length us, event | category | flops | bytes accessed | tf_op | source)
XLA Modules:
  0.0 48.1 jit_solution(12613965564550174397)
XLA Ops:
  1.3 46.0 %shard_map.129 = (bf16[16,32,256]{2,1,0:T(8,128)(2,1)S(1)}, bf16[16,32,256]{2,1,0:T(8,128)(2,1)S(1)}, f32[9,8,16]{2,1,0:T(8,128)S(1)}, bf16[2,4,256]{2,1,0:T(4,128)(2,1)S(1)}) custom-call(s32[1]{0:T(128)S(6)} %copy.14.step_ref, bf16[16,32,256]{2,1,0:T(8,128)(2,1)} %field_hbm.1, bf16[16,32,256]{2,1,0:T(8,128)(2,1)} %cot_hbm.1, bf16[9,256,256]{2,1,0:T(8,128)(2,1)} %taps_hbm.1, ...), custom_call_target="tpu_custom_call" | custom-call | tf_op jit(solution)/shard_map/pallas_call | solution.py:493
  47.3 0.8 %shard_map.130 = (bf16[16,32,256]{2,1,0:T(8,128)(2,1)}, bf16[16,32,256]{2,1,0:T(8,128)(2,1)}, f32[9,8,16]{2,1,0:T(8,128)}, bf16[2,4,256]{2,1,0:T(4,128)(2,1)}) custom-call(bf16[16,32,256]{2,1,0:T(8,128)(2,1)S(1)} %get-tuple-element.8.refs_0_, bf16[16,32,256]{2,1,0:T(8,128)(2,1)S(1)} %get-tuple-element.9.refs_1_, f32[9,8,16]{2,1,0:T(8,128)S(1)} %get-tuple-element.10.refs_2_, ...), custom_call_target="tpu_custom_call" | custom-call | tf_op jit(solution)/shard_map/pallas_call | solution.py:423

commit v5 on v4

--- a/solution.py
+++ b/solution.py
@@ -148,7 +148,7 @@
     other = (lat, lon + 1 - 2 * core)
 
     barrier = pltpu.get_barrier_semaphore()
-    everyone = near + [plane(k, 1) for k in range(NPLANE)] + [ring(*d) for d in LINE]
+    everyone = near + [ring(*d) for d in LINE] + [plane(k, 1) for k in SPREAD]
     for dev in everyone:
         pl.semaphore_signal(barrier, inc=1, device_id=dev, device_id_type=MESH)
     for load in loads:
@@ -290,16 +290,6 @@
     for k in SPREAD:
         send(q_buf.at[NPLANE], q_buf.at[k], group_s.at[1], group_r.at[1], plane(k, 1))
 
-    for b in range(3):
-        win_cot[b] = pad_cot[:, 7 + b : 7 + b + COLS, :].astype(BF16)
-    back = jnp.zeros((CELLS, C), F32)
-    for tap in range(9):
-        back = back + dot_t(window(win_cot, 2 - tap // 3, 2 - tap % 3), taps[tap])
-    sig = 1.0 / (1.0 + jnp.exp(-xf))
-    grad_field[...] = (
-        (flat_cot.astype(F32) + back * sig * (1.0 + xf * (1.0 - sig))).astype(BF16).reshape(ROWS, COLS, C)
-    )
-
     await_recv(x_in_p, group_s.at[3], group_r.at[3], other)
     acc = x_out_p[x].astype(F32)
     for k in range(NX - 1):
@@ -317,6 +307,16 @@
     for k in (2, 1, 3):
         to = (x + k) % NX
         send(x_out_q.at[to], x_in_q.at[k - 1], group_s.at[9], group_r.at[9], device(y, z, to, core))
+
+    for b in range(3):
+        win_cot[b] = pad_cot[:, 7 + b : 7 + b + COLS, :].astype(BF16)
+    back = jnp.zeros((CELLS, C), F32)
+    for tap in range(9):
+        back = back + dot_t(window(win_cot, 2 - tap // 3, 2 - tap % 3), taps[tap])
+    sig = 1.0 / (1.0 + jnp.exp(-xf))
+    grad_field[...] = (
+        (flat_cot.astype(F32) + back * sig * (1.0 + xf * (1.0 - sig))).astype(BF16).reshape(ROWS, COLS, C)
+    )
 
     await_recv(y_in_p, group_s.at[5], group_r.at[5], other)
     await_recv(x_in_q, group_s.at[9], group_r.at[9], other)

time: 48.3 us -> 48 us (level)
  no operation moved by 1% of the time
where the time goes in v5:
time: 48 us; the launch traced here: 47.8 us
  Pallas kernels  46.5 us (97%)
  between operations  1.29 us (3%)
    pallas_call x1, Pallas kernels, shards(): call(timestep, *(pltpu.with_memory_space_constraint(v, pltpu.HBM) for v i...  45.7 us

profile of v5, /device:TPU:1, one launch (start us, length us, event | category | flops | bytes accessed | tf_op | source)
XLA Modules:
  0.0 47.8 jit_solution(16730358272670220080)
XLA Ops:
  1.3 45.7 %shard_map.129 = (bf16[16,32,256]{2,1,0:T(8,128)(2,1)S(1)}, bf16[16,32,256]{2,1,0:T(8,128)(2,1)S(1)}, f32[9,8,16]{2,1,0:T(8,128)S(1)}, bf16[2,4,256]{2,1,0:T(4,128)(2,1)S(1)}) custom-call(s32[1]{0:T(128)S(6)} %copy.14.step_ref, bf16[16,32,256]{2,1,0:T(8,128)(2,1)} %field_hbm.1, bf16[16,32,256]{2,1,0:T(8,128)(2,1)} %cot_hbm.1, bf16[9,256,256]{2,1,0:T(8,128)(2,1)} %taps_hbm.1, ...), custom_call_target="tpu_custom_call" | custom-call | tf_op jit(solution)/shard_map/pallas_call | solution.py:493
  47.0 0.8 %shard_map.130 = (bf16[16,32,256]{2,1,0:T(8,128)(2,1)}, bf16[16,32,256]{2,1,0:T(8,128)(2,1)}, f32[9,8,16]{2,1,0:T(8,128)}, bf16[2,4,256]{2,1,0:T(4,128)(2,1)}) custom-call(bf16[16,32,256]{2,1,0:T(8,128)(2,1)S(1)} %get-tuple-element.8.refs_0_, bf16[16,32,256]{2,1,0:T(8,128)(2,1)S(1)} %get-tuple-element.9.refs_1_, f32[9,8,16]{2,1,0:T(8,128)S(1)} %get-tuple-element.10.refs_2_, ...), custom_call_target="tpu_custom_call" | custom-call | tf_op jit(solution)/shard_map/pallas_call | solution.py:423

commit v6 on v5

--- a/solution.py
+++ b/solution.py
@@ -148,7 +148,8 @@
     other = (lat, lon + 1 - 2 * core)
 
     barrier = pltpu.get_barrier_semaphore()
-    everyone = near + [ring(*d) for d in LINE] + [plane(k, 1) for k in SPREAD]
+    everyone = near + [ring(*d) for d in LINE if d != (0, 1)]
+    everyone += [plane(k, 1) for k in SPREAD if PLANE[k] != (0, 0, 1)]
     for dev in everyone:
         pl.semaphore_signal(barrier, inc=1, device_id=dev, device_id_type=MESH)
     for load in loads:

time: 48 us -> 48 us (level)
  no operation moved by 1% of the time
where the time goes in v6:
time: 48 us; the launch traced here: 47.8 us
  Pallas kernels  46.5 us (97%)
  between operations  1.29 us (3%)
    pallas_call x1, Pallas kernels, shards(): call(timestep, *(pltpu.with_memory_space_constraint(v, pltpu.HBM) for v i...  45.7 us

profile of v6, /device:TPU:1, one launch (start us, length us, event | category | flops | bytes accessed | tf_op | source)
XLA Modules:
  0.0 47.8 jit_solution(10067802006422652607)
XLA Ops:
  1.3 45.7 %shard_map.129 = (bf16[16,32,256]{2,1,0:T(8,128)(2,1)S(1)}, bf16[16,32,256]{2,1,0:T(8,128)(2,1)S(1)}, f32[9,8,16]{2,1,0:T(8,128)S(1)}, bf16[2,4,256]{2,1,0:T(4,128)(2,1)S(1)}) custom-call(s32[1]{0:T(128)S(6)} %copy.14.step_ref, bf16[16,32,256]{2,1,0:T(8,128)(2,1)} %field_hbm.1, bf16[16,32,256]{2,1,0:T(8,128)(2,1)} %cot_hbm.1, bf16[9,256,256]{2,1,0:T(8,128)(2,1)} %taps_hbm.1, ...), custom_call_target="tpu_custom_call" | custom-call | tf_op jit(solution)/shard_map/pallas_call | solution.py:494
  47.0 0.8 %shard_map.130 = (bf16[16,32,256]{2,1,0:T(8,128)(2,1)}, bf16[16,32,256]{2,1,0:T(8,128)(2,1)}, f32[9,8,16]{2,1,0:T(8,128)}, bf16[2,4,256]{2,1,0:T(4,128)(2,1)}) custom-call(bf16[16,32,256]{2,1,0:T(8,128)(2,1)S(1)} %get-tuple-element.8.refs_0_, bf16[16,32,256]{2,1,0:T(8,128)(2,1)S(1)} %get-tuple-element.9.refs_1_, f32[9,8,16]{2,1,0:T(8,128)S(1)} %get-tuple-element.10.refs_2_, ...), custom_call_target="tpu_custom_call" | custom-call | tf_op jit(solution)/shard_map/pallas_call | solution.py:424
